TPU v7x, 256 devices: a whole 4x4x8 slice. The times are simulated.
256 devices in a mesh: slab: 16 (over z, core), clus: 16 (over y, x).
Axes of the slice: x: 4, y: 4, z: 8, core: 2. Of those that a mesh axis runs over, the one named last changes fastest.
Arguments:
- incident: float32 [8, 1024, 200], P(None, ('slab', 'clus')), may hold values from -6 to 6
- history: float32 [16, 1024, 200], P(None, ('slab', 'clus')), may hold values from -6 to 6
- near_blocks: bfloat16 [1024, 12, 200, 200], P(('slab', 'clus')), may hold values from -0.09375 to 0.09375
- near_idx: int32 [1024, 12], P(('slab', 'clus')), may hold values from 0 to 1023, as said below
- near_cnt: int32 [1024], P(('slab', 'clus')), may hold values from 3 to 12
- near_lag: int32 [1024, 12], P(('slab', 'clus')), may hold values from 1 to 15
- near_frac: float32 [1024, 12], P(('slab', 'clus')), may hold values from 0 to 1
- inverses: bfloat16 [1024, 200, 200], P(('slab', 'clus')), may hold values from -0.4375 to 0.4375
- rays: bfloat16 [1024, 512, 200], P(('slab', 'clus')), may hold values from -0.4375 to 0.4375
- shift: float32 [1024, 512], P(('slab', 'clus')), may hold values from -1 to 1
- far_idx: int32 [256, 8], replicated, may hold values from 0 to 255, as said below
- far_lag: int32 [256, 8], replicated, may hold values from 1 to 16
- trans: bfloat16 [256, 8, 512], replicated, may hold values from -0.5 to 0.5
Outputs:
- currents: float32 [8, 1024, 200], P(None, ('slab', 'clus'))
Inputs may be any that keep to these rules, and one draw needn't show every extreme that they name: `near_idx`: every entry is a cluster whose slab (cluster number divided by 64) differs by at most one from the slab of the entry's row. `far_idx`: every entry is a group whose slab (group number divided by the number of devices along clus) differs by two or more from the slab of the entry's row.
All inputs are finite; a program needn't handle non-finite values.
Results may differ from a plain program's by a relative error of at most 0.0045.
Values sent between devices are 32-bit elements; how exact they have to be, the bound alone decides.
A program may use at most 128 MiB of HBM per device.

v0:
```python
import jax
import jax.numpy as jnp
from jax import lax
from jax.sharding import PartitionSpec as P


def extended(block, sides, width):
    for axis, dim in sides:
        count = lax.axis_size(axis)
        forward = [(i, i + 1) for i in range(count - 1)]
        backward = [(target, source) for source, target in forward]
        low = lax.ppermute(
            lax.slice_in_dim(block, block.shape[dim] - width, None, axis=dim), axis, forward
        )
        high = lax.ppermute(lax.slice_in_dim(block, 0, width, axis=dim), axis, backward)
        block = jnp.concatenate([low, block, high], axis=dim)
    return block


def project_out(rays, shift, current):
    ray_vals = jnp.einsum(
        "cdu,cu->cd", rays, current.astype(jnp.bfloat16), preferred_element_type=jnp.float32
    )
    return jnp.sum(ray_vals * shift, axis=0)


def widen_history(history, slab_size):
    gathered = lax.all_gather(history, "clus", axis=1, tiled=True)
    return extended(gathered, (("slab", 1),), slab_size)


def widen_step(current, slab_size):
    gathered = lax.all_gather(current, "clus", axis=0, tiled=True)
    return extended(gathered, (("slab", 0),), slab_size)


def local(
    incident,
    history,
    near_blocks,
    near_idx,
    near_cnt,
    near_lag,
    near_frac,
    inverses,
    rays,
    shift,
    far_idx,
    far_lag,
    trans,
):
    lag_count = history.shape[0]
    step_count = incident.shape[0]
    local_count = history.shape[1]
    dir_count = rays.shape[1]
    slab_count = lax.axis_size("slab")
    clus_count = lax.axis_size("clus")
    slab_size = local_count * clus_count
    group_count = slab_count * clus_count
    slab_index = lax.axis_index("slab")
    myself = slab_index * clus_count + lax.axis_index("clus")
    near_local = near_idx - (slab_index - 1) * slab_size
    neighbours = widen_history(history, slab_size)
    near_time = jnp.concatenate(
        [neighbours, jnp.zeros((step_count,) + neighbours.shape[1:], jnp.float32)], axis=0
    )
    hist_rays = jnp.einsum(
        "cdu,tcu->tcd", rays, history.astype(jnp.bfloat16), preferred_element_type=jnp.float32
    )
    own_hist = jnp.sum(hist_rays * shift[None], axis=1)
    own_time = jnp.concatenate([own_hist, jnp.zeros((step_count, dir_count), jnp.float32)], axis=0)
    spectra_all = lax.all_gather(own_hist[:, None, :], ("slab", "clus"), axis=1, tiled=True)
    spectra_all = jnp.concatenate(
        [spectra_all, jnp.zeros((step_count, group_count, dir_count), jnp.float32)], axis=0
    )
    idx_row = lax.dynamic_index_in_dim(far_idx, myself, 0, keepdims=False)
    lag_row = lax.dynamic_index_in_dim(far_lag, myself, 0, keepdims=False)
    trans_row = lax.dynamic_index_in_dim(trans, myself, 0, keepdims=False).astype(jnp.float32)
    live_slot = jnp.arange(near_idx.shape[1])[None, :] < near_cnt[:, None]
    near_weight = near_frac[..., None]
    outputs = []
    for step_index in range(step_count):
        lag_slot = step_index - near_lag + lag_count
        first_lag = near_time[lag_slot, near_local]
        second = near_time[lag_slot - 1, near_local]
        blended = jnp.where(
            live_slot[..., None], (1.0 - near_weight) * first_lag + near_weight * second, 0.0
        ).astype(jnp.bfloat16)
        near_field = jnp.einsum(
            "cjuv,cjv->cu", near_blocks, blended, preferred_element_type=jnp.float32
        )
        picked = spectra_all[step_index - lag_row + lag_count, idx_row]
        incoming = jnp.sum(trans_row * picked, axis=0)
        inbound = (shift * incoming[None, :]).astype(jnp.bfloat16)
        far_field = jnp.einsum("cdu,cd->cu", rays, inbound, preferred_element_type=jnp.float32)
        right_side = (incident[step_index] - near_field - far_field).astype(jnp.bfloat16)
        current = jnp.einsum("cuv,cv->cu", inverses, right_side, preferred_element_type=jnp.float32)
        outputs.append(current)
        if step_index + 1 < step_count:
            spectrum = project_out(rays, shift, current)
            own_time = own_time.at[lag_count + step_index].set(spectrum)
            near_time = near_time.at[lag_count + step_index].set(widen_step(current, slab_size))
            fresh_rays = lax.all_gather(spectrum[None, :], ("slab", "clus"), axis=0, tiled=True)
            spectra_all = spectra_all.at[lag_count + step_index].set(fresh_rays)
    return jnp.stack(outputs, axis=0)


def solution(mesh):
    in_specs = (
        P(None, ("slab", "clus"), None),
        P(None, ("slab", "clus"), None),
        P(("slab", "clus"), None, None, None),
        P(("slab", "clus"), None),
        P(("slab", "clus")),
        P(("slab", "clus"), None),
        P(("slab", "clus"), None),
        P(("slab", "clus"), None, None),
        P(("slab", "clus"), None, None),
        P(("slab", "clus"), None),
        P(),
        P(),
        P(),
    )
    out_specs = P(None, ("slab", "clus"), None)
    return jax.shard_map(local, mesh=mesh, in_specs=in_specs, out_specs=out_specs, check_vma=False)
```

profile of v0, /device:TPU:1, one launch (start us, length us, event | category | flops | bytes accessed | tf_op | source)
XLA Modules:
  0.0 1253.5 jit_solution(12434369573532514118)
XLA Ops:
  7.7 1.5 fusion
  10.1 21.2 %all_gather.48 = f32[16,64,200]{2,0,1:T(8,128)S(1)} all-gather(f32[16,4,200]{2,0,1:T(8,128)S(1)} %copy.16), channel_id=1, replica_groups=mesh['slab'=16,'clus'=16] {'clus'}, dimensions={1}, use_global_device_ids=true | all-gather | bytes 870400 | tf_op jit(solution)/shard_map/all_gather | solution.py:28
  31.9 9.0 collective-permute-start
  40.9 1.9 collective-permute-start.1
  46.9 6.1 collective-permute-done
  53.0 4.4 collective-permute-done.1
  57.4 3.8 select_maximum_fusion
  61.2 2.1 gather_fusion
  63.4 2.1 gather_fusion.1
  65.6 3.7 fusion.22
  69.4 64.4 %all-gather.24.cloned.1.call-done = f32[16,131072]{1,0:T(8,128)} async-done(((f32[16,512]{1,0:T(8,128)}), f32[16,131072]{1,0:T(8,128)}) %all-gather.24.cloned.1.call-update) | async-done | bytes 8388624 | tf_op jit(solution)/shard_map/all_gather | solution.py:72
  133.8 8.2 copy.90
  142.0 6.7 concatenate.120
  151.3 17.8 %all-gather.8 = f32[16,4,200]{2,1,0:T(4,128)S(1)} all-gather(f32[1,4,200]{2,1,0:T(4,128)S(1)} %bitcast.498), channel_id=1, replica_groups=mesh['slab'=16,'clus'=16] {'clus'}, dimensions={0}, use_global_device_ids=true | all-gather | bytes 54400 | tf_op jit(solution)/shard_map/all_gather | solution.py:33
  169.1 7.5 collective-permute-start.2
  176.6 1.9 collective-permute-start.3
  178.8 114.5 %all-gather.9 = f32[256,1,512]{2,1,0:T(1,128)S(1)} all-gather(f32[1,1,512]{2,1,0:T(1,128)S(1)} %bitcast.505), channel_id=3, replica_groups=mesh['slab'=16,'clus'=16] {'slab','clus'}, dimensions={0}, use_global_device_ids=true | all-gather | bytes 526336 | tf_op jit(solution)/shard_map/all_gather | solution.py:103
  297.1 2.1 gather_fusion.4
  299.3 2.1 gather_fusion.3
  301.5 3.7 fusion.20
  305.5 16.8 %all-gather.10 = f32[16,4,200]{2,1,0:T(4,128)S(1)} all-gather(f32[1,4,200]{2,1,0:T(4,128)S(1)} %bitcast.499), channel_id=1, replica_groups=mesh['slab'=16,'clus'=16] {'clus'}, dimensions={0}, use_global_device_ids=true | all-gather | bytes 54400 | tf_op jit(solution)/shard_map/all_gather | solution.py:33
  322.4 7.2 collective-permute-start.4
  329.5 3.2 collective-permute-start.5
  333.0 114.1 %all-gather.11 = f32[256,1,512]{2,1,0:T(1,128)S(1)} all-gather(f32[1,1,512]{2,1,0:T(1,128)S(1)} %bitcast.506), channel_id=4, replica_groups=mesh['slab'=16,'clus'=16] {'slab','clus'}, dimensions={0}, use_global_device_ids=true | all-gather | bytes 526336 | tf_op jit(solution)/shard_map/all_gather | solution.py:103
  447.9 1.3 gather_fusion.8
  451.0 2.1 gather_fusion.7
  453.1 2.1 gather_fusion.6
  455.4 3.7 fusion.18
  459.4 17.1 %all-gather.12 = f32[16,4,200]{2,1,0:T(4,128)S(1)} all-gather(f32[1,4,200]{2,1,0:T(4,128)S(1)} %bitcast.500), channel_id=1, replica_groups=mesh['slab'=16,'clus'=16] {'clus'}, dimensions={0}, use_global_device_ids=true | all-gather | bytes 54400 | tf_op jit(solution)/shard_map/all_gather | solution.py:33
  476.5 7.8 collective-permute-start.6
  484.3 1.9 collective-permute-start.7
  486.5 118.1 %all-gather.13 = f32[256,1,512]{2,1,0:T(1,128)S(1)} all-gather(f32[1,1,512]{2,1,0:T(1,128)S(1)} %bitcast.507), channel_id=5, replica_groups=mesh['slab'=16,'clus'=16] {'slab','clus'}, dimensions={0}, use_global_device_ids=true | all-gather | bytes 526336 | tf_op jit(solution)/shard_map/all_gather | solution.py:103
  608.5 2.1 gather_fusion.10
  610.6 2.1 gather_fusion.9
  612.9 3.7 fusion.16
  616.9 16.1 %all-gather.14 = f32[16,4,200]{2,1,0:T(4,128)S(1)} all-gather(f32[1,4,200]{2,1,0:T(4,128)S(1)} %bitcast.501), channel_id=1, replica_groups=mesh['slab'=16,'clus'=16] {'clus'}, dimensions={0}, use_global_device_ids=true | all-gather | bytes 54400 | tf_op jit(solution)/shard_map/all_gather | solution.py:33
  633.0 9.1 collective-permute-start.8
  642.0 1.9 collective-permute-start.9
  644.2 116.6 %all-gather.15 = f32[256,1,512]{2,1,0:T(1,128)S(1)} all-gather(f32[1,1,512]{2,1,0:T(1,128)S(1)} %bitcast.508), channel_id=6, replica_groups=mesh['slab'=16,'clus'=16] {'slab','clus'}, dimensions={0}, use_global_device_ids=true | all-gather | bytes 526336 | tf_op jit(solution)/shard_map/all_gather | solution.py:103
  764.7 2.1 gather_fusion.13
  766.9 2.1 gather_fusion.12
  769.1 3.7 fusion.14
  773.1 18.0 %all-gather.16 = f32[16,4,200]{2,1,0:T(4,128)S(1)} all-gather(f32[1,4,200]{2,1,0:T(4,128)S(1)} %bitcast.502), channel_id=1, replica_groups=mesh['slab'=16,'clus'=16] {'clus'}, dimensions={0}, use_global_device_ids=true | all-gather | bytes 54400 | tf_op jit(solution)/shard_map/all_gather | solution.py:33
  791.1 7.5 collective-permute-start.10
  798.6 1.9 collective-permute-start.11
  800.8 118.5 %all-gather.17 = f32[256,1,512]{2,1,0:T(1,128)S(1)} all-gather(f32[1,1,512]{2,1,0:T(1,128)S(1)} %bitcast.509), channel_id=7, replica_groups=mesh['slab'=16,'clus'=16] {'slab','clus'}, dimensions={0}, use_global_device_ids=true | all-gather | bytes 526336 | tf_op jit(solution)/shard_map/all_gather | solution.py:103
  920.2 1.3 gather_fusion.17
  923.2 2.1 gather_fusion.16
  925.3 2.1 gather_fusion.15
  927.6 3.7 fusion.12
  931.6 15.8 %all-gather.18 = f32[16,4,200]{2,1,0:T(4,128)S(1)} all-gather(f32[1,4,200]{2,1,0:T(4,128)S(1)} %bitcast.503), channel_id=1, replica_groups=mesh['slab'=16,'clus'=16] {'clus'}, dimensions={0}, use_global_device_ids=true | all-gather | bytes 54400 | tf_op jit(solution)/shard_map/all_gather | solution.py:33
  947.4 9.4 collective-permute-start.12
  956.8 1.9 collective-permute-start.13
  958.9 116.6 %all-gather.19 = f32[256,1,512]{2,1,0:T(1,128)S(1)} all-gather(f32[1,1,512]{2,1,0:T(1,128)S(1)} %bitcast.510), channel_id=8, replica_groups=mesh['slab'=16,'clus'=16] {'slab','clus'}, dimensions={0}, use_global_device_ids=true | all-gather | bytes 526336 | tf_op jit(solution)/shard_map/all_gather | solution.py:103
  1079.5 2.1 gather_fusion.19
  1081.6 2.1 gather_fusion.18
  1083.9 3.7 fusion.10
  1087.8 17.7 %all-gather.20 = f32[16,4,200]{2,1,0:T(4,128)S(1)} all-gather(f32[1,4,200]{2,1,0:T(4,128)S(1)} %bitcast.504), channel_id=1, replica_groups=mesh['slab'=16,'clus'=16] {'clus'}, dimensions={0}, use_global_device_ids=true | all-gather | bytes 54400 | tf_op jit(solution)/shard_map/all_gather | solution.py:33
  1105.6 7.5 collective-permute-start.14
  1113.1 1.9 collective-permute-start.15
  1115.3 118.5 %all-gather.21 = f32[256,1,512]{2,1,0:T(1,128)S(1)} all-gather(f32[1,1,512]{2,1,0:T(1,128)S(1)} %bitcast.511), channel_id=9, replica_groups=mesh['slab'=16,'clus'=16] {'slab','clus'}, dimensions={0}, use_global_device_ids=true | all-gather | bytes 526336 | tf_op jit(solution)/shard_map/all_gather | solution.py:103
  1237.7 2.1 gather_fusion.22
  1239.8 2.1 gather_fusion.21
  1242.0 3.7 fusion.8
  (172 shorter events, 38.8 us)
Async XLA Ops:
  6.5 1.2 copy-start
  6.5 127.2 %all-gather.24.cloned.1.call-start = ((), (), s32[]{:S(2)}) async-start(), calls=%async_computation | async-start | bytes 8421376 | tf_op jit(solution)/shard_map/all_gather | solution.py:72
  31.9 21.0 %collective-permute-start = (f32[16,64,200]{2,1,0:T(8,128)S(1)}, f32[16,64,200]{2,1,0:T(8,128)S(1)}, u32[]{:S(2)}, u32[]{:S(2)}) collective-permute-start(f32[16,64,200]{2,1,0:T(8,128)S(1)} %copy.17), channel_id=1, source_target_pairs={{0,16},{16,32},{32,48},{48,64},{64,80},{80,96},{96,112},{112,128},... | collective-permute-start | bytes 2457608 | tf_op jit(solution)/shard_map/ppermute | solution.py:12
  40.9 16.5 %collective-permute-start.1 = (f32[16,64,200]{2,1,0:T(8,128)S(1)}, f32[16,64,200]{2,1,0:T(8,128)}, u32[]{:S(2)}, u32[]{:S(2)}) collective-permute-start(f32[16,64,200]{2,1,0:T(8,128)S(1)} %copy.17), channel_id=1, source_target_pairs={{16,0},{32,16},{48,32},{64,48},{80,64},{96,80},{112,96},{128,112},... | collective-permute-start | bytes 2457608 | tf_op jit(solution)/shard_map/ppermute | solution.py:15
  43.8 21.7 %copy-start.3 = (f32[4,12]{1,0:T(4,128)S(1)}, f32[4,12]{1,0:T(4,128)}, u32[]{:S(2)}) copy-start(f32[4,12]{1,0:T(4,128)} %param.47) | copy-start | bytes 580
  142.0 8.7 copy-start.2
  142.0 9.0 copy-start.4
  142.0 9.0 copy-start.1
  169.1 127.3 %collective-permute-start.2 = (f32[64,200]{1,0:T(8,128)S(1)}, f32[64,200]{1,0:T(8,128)S(1)}, u32[]{:S(2)}, u32[]{:S(2)}) collective-permute-start(f32[64,200]{1,0:T(8,128)S(1)} %reshape.947), channel_id=1, source_target_pairs={{0,16},{16,32},{32,48},{48,64},{64,80},{80,96},{96,112},{112,128},... | collective-permute-start | bytes 153608 | tf_op jit(solution)/shard_map/ppermute | solution.py:12
  176.6 119.9 %collective-permute-start.3 = (f32[64,200]{1,0:T(8,128)S(1)}, f32[64,200]{1,0:T(8,128)S(1)}, u32[]{:S(2)}, u32[]{:S(2)}) collective-permute-start(f32[64,200]{1,0:T(8,128)S(1)} %reshape.947), channel_id=1, source_target_pairs={{16,0},{32,16},{48,32},{64,48},{80,64},{96,80},{112,96},{128,112},... | collective-permute-start | bytes 153608 | tf_op jit(solution)/shard_map/ppermute | solution.py:15
  322.4 127.9 %collective-permute-start.4 = (f32[64,200]{1,0:T(8,128)S(1)}, f32[64,200]{1,0:T(8,128)S(1)}, u32[]{:S(2)}, u32[]{:S(2)}) collective-permute-start(f32[64,200]{1,0:T(8,128)S(1)} %reshape.951), channel_id=1, source_target_pairs={{0,16},{16,32},{32,48},{48,64},{64,80},{80,96},{96,112},{112,128},... | collective-permute-start | bytes 153608 | tf_op jit(solution)/shard_map/ppermute | solution.py:12
  329.5 120.8 %collective-permute-start.5 = (f32[64,200]{1,0:T(8,128)S(1)}, f32[64,200]{1,0:T(8,128)S(1)}, u32[]{:S(2)}, u32[]{:S(2)}) collective-permute-start(f32[64,200]{1,0:T(8,128)S(1)} %reshape.951), channel_id=1, source_target_pairs={{16,0},{32,16},{48,32},{64,48},{80,64},{96,80},{112,96},{128,112},... | collective-permute-start | bytes 153608 | tf_op jit(solution)/shard_map/ppermute | solution.py:15
  476.5 131.3 %collective-permute-start.6 = (f32[64,200]{1,0:T(8,128)S(1)}, f32[64,200]{1,0:T(8,128)S(1)}, u32[]{:S(2)}, u32[]{:S(2)}) collective-permute-start(f32[64,200]{1,0:T(8,128)S(1)} %reshape.955), channel_id=1, source_target_pairs={{0,16},{16,32},{32,48},{48,64},{64,80},{80,96},{96,112},{112,128},... | collective-permute-start | bytes 153608 | tf_op jit(solution)/shard_map/ppermute | solution.py:12
  484.3 123.5 %collective-permute-start.7 = (f32[64,200]{1,0:T(8,128)S(1)}, f32[64,200]{1,0:T(8,128)S(1)}, u32[]{:S(2)}, u32[]{:S(2)}) collective-permute-start(f32[64,200]{1,0:T(8,128)S(1)} %reshape.955), channel_id=1, source_target_pairs={{16,0},{32,16},{48,32},{64,48},{80,64},{96,80},{112,96},{128,112},... | collective-permute-start | bytes 153608 | tf_op jit(solution)/shard_map/ppermute | solution.py:15
  633.0 131.1 %collective-permute-start.8 = (f32[64,200]{1,0:T(8,128)S(1)}, f32[64,200]{1,0:T(8,128)S(1)}, u32[]{:S(2)}, u32[]{:S(2)}) collective-permute-start(f32[64,200]{1,0:T(8,128)S(1)} %reshape.959), channel_id=1, source_target_pairs={{0,16},{16,32},{32,48},{48,64},{64,80},{80,96},{96,112},{112,128},... | collective-permute-start | bytes 153608 | tf_op jit(solution)/shard_map/ppermute | solution.py:12
  642.0 122.0 %collective-permute-start.9 = (f32[64,200]{1,0:T(8,128)S(1)}, f32[64,200]{1,0:T(8,128)S(1)}, u32[]{:S(2)}, u32[]{:S(2)}) collective-permute-start(f32[64,200]{1,0:T(8,128)S(1)} %reshape.959), channel_id=1, source_target_pairs={{16,0},{32,16},{48,32},{64,48},{80,64},{96,80},{112,96},{128,112},... | collective-permute-start | bytes 153608 | tf_op jit(solution)/shard_map/ppermute | solution.py:15
  791.1 131.4 %collective-permute-start.10 = (f32[64,200]{1,0:T(8,128)S(1)}, f32[64,200]{1,0:T(8,128)S(1)}, u32[]{:S(2)}, u32[]{:S(2)}) collective-permute-start(f32[64,200]{1,0:T(8,128)S(1)} %reshape.963), channel_id=1, source_target_pairs={{0,16},{16,32},{32,48},{48,64},{64,80},{80,96},{96,112},{112,128},... | collective-permute-start | bytes 153608 | tf_op jit(solution)/shard_map/ppermute | solution.py:12
  798.6 123.9 %collective-permute-start.11 = (f32[64,200]{1,0:T(8,128)S(1)}, f32[64,200]{1,0:T(8,128)S(1)}, u32[]{:S(2)}, u32[]{:S(2)}) collective-permute-start(f32[64,200]{1,0:T(8,128)S(1)} %reshape.963), channel_id=1, source_target_pairs={{16,0},{32,16},{48,32},{64,48},{80,64},{96,80},{112,96},{128,112},... | collective-permute-start | bytes 153608 | tf_op jit(solution)/shard_map/ppermute | solution.py:15
  947.4 131.4 %collective-permute-start.12 = (f32[64,200]{1,0:T(8,128)S(1)}, f32[64,200]{1,0:T(8,128)S(1)}, u32[]{:S(2)}, u32[]{:S(2)}) collective-permute-start(f32[64,200]{1,0:T(8,128)S(1)} %reshape.967), channel_id=1, source_target_pairs={{0,16},{16,32},{32,48},{48,64},{64,80},{80,96},{96,112},{112,128},... | collective-permute-start | bytes 153608 | tf_op jit(solution)/shard_map/ppermute | solution.py:12
  956.8 122.0 %collective-permute-start.13 = (f32[64,200]{1,0:T(8,128)S(1)}, f32[64,200]{1,0:T(8,128)S(1)}, u32[]{:S(2)}, u32[]{:S(2)}) collective-permute-start(f32[64,200]{1,0:T(8,128)S(1)} %reshape.967), channel_id=1, source_target_pairs={{16,0},{32,16},{48,32},{64,48},{80,64},{96,80},{112,96},{128,112},... | collective-permute-start | bytes 153608 | tf_op jit(solution)/shard_map/ppermute | solution.py:15
  1105.6 131.4 %collective-permute-start.14 = (f32[64,200]{1,0:T(8,128)S(1)}, f32[64,200]{1,0:T(8,128)S(1)}, u32[]{:S(2)}, u32[]{:S(2)}) collective-permute-start(f32[64,200]{1,0:T(8,128)S(1)} %reshape.971), channel_id=1, source_target_pairs={{0,16},{16,32},{32,48},{48,64},{64,80},{80,96},{96,112},{112,128},... | collective-permute-start | bytes 153608 | tf_op jit(solution)/shard_map/ppermute | solution.py:12
  1113.1 123.9 %collective-permute-start.15 = (f32[64,200]{1,0:T(8,128)S(1)}, f32[64,200]{1,0:T(8,128)S(1)}, u32[]{:S(2)}, u32[]{:S(2)}) collective-permute-start(f32[64,200]{1,0:T(8,128)S(1)} %reshape.971), channel_id=1, source_target_pairs={{16,0},{32,16},{48,32},{64,48},{80,64},{96,80},{112,96},{128,112},... | collective-permute-start | bytes 153608 | tf_op jit(solution)/shard_map/ppermute | solution.py:15
  1236.9 8.9 copy-start.5
Sparse Core Ops, SparseCore 0:
  11.0 122.7 all-gather.23
where the time goes:
time: 1260 us; the launch traced here: 1250 us
  blocking collectives  957 us (76%)
  starting transfers between devices  81.5 us (6%)
  waiting for transfers between devices  75 us (6%)
  local copies, waits for them, and re-layouts  68.7 us (5%)
  matrix products  37.2 us (3%)
  other arithmetic  19.7 us (2%)
  between operations  14.1 us (1%)
    all_gather x7, blocking collectives, local(): lax.all_gather(spectrum[None, :], ('slab', 'clus'), axis=0, tiled=True)  817 us
    all_gather x7, blocking collectives, widen_step(): gathered = lax.all_gather(current, 'clus', axis=0, tiled=True)  119 us
    ppermute x8, starting transfers between devices, extended(): lax.ppermute(lax.slice_in_dim(block, block.shape[dim] - width, None, axis...  64.9 us
    all_gather x1, waiting for transfers between devices, local(): lax.all_gather(own_hist[:, None, :], ('slab', 'clus'), axis=1, tiled=True)  64.4 us
    dot_general x8, matrix products, local(): jnp.einsum('cjuv,cjv->cu', near_blocks, blended, preferred_element_type=j...  29.9 us
  transfers between devices with their start and end apart: 17, of which 3 were waited for; matrix products, arithmetic and copies ran while one was open for 3% of the time, Pallas kernels for 0%

commit v1 on v0

v1 whole, which is shorter than its diff:
```python
import functools

import jax
import jax.numpy as jnp
from jax import lax
from jax.experimental import pallas as pl
from jax.experimental.pallas import tpu as pltpu
from jax.sharding import PartitionSpec as P

MESH = pl.DeviceIdType.MESH
LANES = 128
CHUNK = 32
NT = (((1,), (1,)), ((), ()))
NN = (((1,), (0,)), ((), ()))


def dot(left, right, dims):
    return lax.dot_general(left, right, dims, preferred_element_type=jnp.float32)


def remote(src, dst, send, recv, device):
    return pltpu.make_async_remote_copy(
        src_ref=src, dst_ref=dst, send_sem=send, recv_sem=recv,
        device_id=device, device_id_type=MESH,
    )


def march(
    sizes,
    near_row, near_sub, near_now, near_old, far_row,
    incident, message0, rays, shift, inverses, far_weight, fresh_weight, near_hbm,
    out,
    near, line, land, spectra, part_out, part_in, early, blend, partial, incoming,
    near_sem, hist_send, hist_recv, wide_send, wide_recv,
    one_send, one_recv, fwd_send, fwd_recv, two_send, two_recv,
):
    steps, lags, n_slab, n_clus, per, slots, unknowns, far_slots = sizes
    span = lags + steps
    slab = lax.axis_index("slab")
    clus = lax.axis_index("clus")
    after = lax.rem(slab + 1, n_slab)
    before = lax.rem(slab + n_slab - 1, n_slab)
    tail = unknowns - LANES
    quarters = shift.shape[1] // LANES
    home = n_clus + clus

    fetch = pltpu.make_async_copy(near_hbm, near, near_sem)
    fetch.start()

    barrier = pltpu.get_barrier_semaphore()

    def greet_plane(k, carry):
        pl.semaphore_signal(barrier, inc=1, device_id=(slab, lax.rem(clus + k, n_clus)), device_id_type=MESH)
        return carry

    def greet_column(k, carry):
        pl.semaphore_signal(barrier, inc=1, device_id=(lax.rem(slab + k, n_slab), clus), device_id_type=MESH)
        return carry

    lax.fori_loop(1, n_clus, greet_plane, 0)
    lax.fori_loop(1, n_slab, greet_column, 0)
    line[home, pl.ds(0, lags)] = message0[...]
    pl.semaphore_wait(barrier, n_clus + n_slab - 2)

    def hist_start(k, carry):
        piece = line.at[home, pl.ds(0, lags)]
        remote(piece, piece, hist_send, hist_recv.at[clus], (slab, lax.rem(clus + k, n_clus))).start()
        return carry

    lax.fori_loop(1, n_clus, hist_start, 0)

    def wide_start(k):
        source = n_clus + k
        piece = line.at[source, pl.ds(0, lags), pl.ds(0, 2)]
        remote(piece, line.at[k + 2 * n_clus, pl.ds(0, lags), pl.ds(0, 2)],
               wide_send.at[0], wide_recv.at[0], (before, clus)).start()
        remote(piece, line.at[k, pl.ds(0, lags), pl.ds(0, 2)],
               wide_send.at[1], wide_recv.at[1], (after, clus)).start()

    wide_start(clus)

    def hist_next(k, carry):
        source = lax.rem(clus + k, n_clus)
        piece = line.at[n_clus + source, pl.ds(0, lags)]
        remote(piece, piece, hist_send, hist_recv.at[source], (slab, clus)).wait_recv()
        wide_start(source)
        return carry

    lax.fori_loop(1, n_clus, hist_next, 0)

    def whole_wide(which):
        piece = line.at[pl.ds(0, n_clus), pl.ds(0, lags), pl.ds(0, 2)]
        return remote(piece, piece, wide_send.at[which], wide_recv.at[which], (slab, clus))

    def far_early(step):
        def one(target, carry):
            total = jnp.zeros((quarters, LANES), jnp.float32)
            for slot in range(far_slots):
                entry = target * far_slots + slot
                row = far_row[step * (n_slab * far_slots) + entry]
                total += far_weight[entry] * line[lax.div(row, span), lax.rem(row, span), 2]
            early[target] = total
            return carry

        lax.fori_loop(0, n_slab, one, 0)

    whole_wide(0).wait_recv()
    whole_wide(1).wait_recv()
    far_early(0)
    fetch.wait()

    row_id = lax.broadcasted_iota(jnp.int32, (per, 1), 0)

    def whole_one(step):
        piece = land.at[step, pl.ds(0, n_clus - 1)]
        return remote(piece, piece, one_send.at[step], one_recv.at[step], (slab, clus))

    def whole_fwd(step, which):
        piece = land.at[step, pl.ds(0, n_clus), pl.ds(0, 2)]
        return remote(piece, piece, fwd_send.at[step, which], fwd_recv.at[step, which], (slab, clus))

    def whole_two(step):
        piece = part_in.at[step, pl.ds(0, n_slab - 1)]
        return remote(piece, piece, two_send.at[step], two_recv.at[step], (slab, clus))

    def body(step, carry):
        totals = [
            jnp.concatenate([early[2 * p], early[2 * p + 1]], axis=0) for p in range(n_slab // 2)
        ]
        for member in range(n_clus):
            one = line[n_clus + member, lags - 1 + step, 2]
            both = jnp.concatenate([one, one], axis=0)
            for p in range(n_slab // 2):
                totals[p] += fresh_weight[member, p] * both
        for p in range(n_slab // 2):
            part_out[step, 2 * p] = totals[p][:quarters]
            part_out[step, 2 * p + 1] = totals[p][quarters:]

        def two_start(k, inner):
            target = lax.rem(slab + k, n_slab)
            remote(part_out.at[step, target], part_in.at[step, slab],
                   two_send.at[step], two_recv.at[step], (target, clus)).start()
            return inner

        lax.fori_loop(1, n_slab, two_start, 0)
        part_in[step, slab] = part_out[step, slab]

        @pl.when(step > 0)
        def _():
            past = step - 1
            for which, first in ((0, 2 * n_clus), (1, 0)):
                whole_fwd(past, which).wait_recv()
                for k in range(n_clus):
                    line[first + k, lags + past, pl.ds(0, 2)] = land[past, first + k, pl.ds(0, 2)]

        def blend_one(entry, inner):
            row = near_row[step * (per * slots) + entry]
            sub = near_sub[entry]
            device, time = lax.div(row, span), lax.rem(row, span)
            now, old = near_now[entry], near_old[entry]
            for half in range(2):
                mixed = (
                    now * line[device, time + 1, half, pl.ds(sub, 1), :]
                    + old * line[device, time, half, pl.ds(sub, 1), :]
                )
                blend[half, pl.ds(entry, 1), :] = mixed.astype(jnp.bfloat16).astype(jnp.float32)
            return inner

        lax.fori_loop(0, per * slots, blend_one, 0, unroll=4)

        def near_one(c, inner):
            for first in range(0, unknowns, CHUNK):
                rows = min(CHUNK, unknowns - first)
                left = jnp.zeros((rows, LANES), jnp.float32)
                right = jnp.zeros((rows, tail), jnp.float32)
                for j in range(slots):
                    entry = c * slots + j
                    left += (near[c, j, pl.ds(first, rows), pl.ds(0, LANES)].astype(jnp.float32)
                             * blend[0, pl.ds(entry, 1), :])
                    right += (near[c, j, pl.ds(first, rows), pl.ds(LANES, tail)].astype(jnp.float32)
                              * blend[1, pl.ds(entry, 1), pl.ds(0, tail)])
                partial[c, pl.ds(first, rows), :] = left + jnp.concatenate(
                    [right, jnp.zeros((rows, LANES - tail), jnp.float32)], axis=1)
            return inner

        lax.fori_loop(0, per, near_one, 0)

        field = jnp.zeros((per, unknowns), jnp.float32)
        for c in range(per):
            pick = jnp.where(row_id == c, 1.0, 0.0) * jnp.ones((per, LANES), jnp.float32)
            pick = pick.astype(jnp.bfloat16)
            value = partial[c]
            high = value.astype(jnp.bfloat16)
            low = (value - high.astype(jnp.float32)).astype(jnp.bfloat16)
            field += dot(pick, high, NT) + dot(pick, low, NT)

        whole_two(step).wait_recv()
        incoming[...] = jnp.sum(part_in[step], axis=0)
        spread = jnp.concatenate(
            [shift[:, q * LANES:(q + 1) * LANES] * incoming[pl.ds(q, 1), :] for q in range(quarters)], axis=1)
        for c in range(per):
            field += dot(jnp.where(row_id == c, spread, 0.0).astype(jnp.bfloat16), rays[c], NN)
        right_side = (incident[step] - field).astype(jnp.bfloat16).astype(jnp.float32)
        current = jnp.zeros((per, unknowns), jnp.float32)
        for c in range(per):
            current += dot(jnp.where(row_id == c, right_side, 0.0).astype(jnp.bfloat16), inverses[c], NT)
        out[step] = current

        @pl.when(step < steps - 1)
        def _():
            rounded = current.astype(jnp.bfloat16).astype(jnp.float32)
            values = jnp.zeros((per, quarters * LANES), jnp.float32)
            for c in range(per):
                values += dot(jnp.where(row_id == c, rounded, 0.0).astype(jnp.bfloat16), rays[c], NT)
            spectrum = jnp.sum(values * shift[...], axis=0, keepdims=True)
            land[step, home, 0] = current[:, :LANES]
            land[step, home, 1] = jnp.concatenate(
                [current[:, LANES:], jnp.zeros((per, LANES - tail), jnp.float32)], axis=1)
            for q in range(quarters):
                land[step, home, 2, pl.ds(q, 1), :] = spectrum[:, q * LANES:(q + 1) * LANES]

            def one_start(k, inner):
                piece = land.at[step, home]
                remote(piece, piece, one_send.at[step], one_recv.at[step],
                       (slab, lax.rem(clus + k, n_clus))).start()
                return inner

            lax.fori_loop(1, n_clus, one_start, 0)
            far_early(step + 1)
            whole_one(step).wait_recv()
            piece = land.at[step, pl.ds(n_clus, n_clus), pl.ds(0, 2)]
            remote(piece, land.at[step, pl.ds(2 * n_clus, n_clus), pl.ds(0, 2)],
                   fwd_send.at[step, 0], fwd_recv.at[step, 0], (before, clus)).start()
            remote(piece, land.at[step, pl.ds(0, n_clus), pl.ds(0, 2)],
                   fwd_send.at[step, 1], fwd_recv.at[step, 1], (after, clus)).start()
            for k in range(n_clus):
                line[n_clus + k, lags + step] = land[step, n_clus + k]

        return carry

    lax.fori_loop(0, steps, body, 0)

    piece = line.at[pl.ds(0, n_clus - 1), pl.ds(0, lags)]
    remote(piece, piece, hist_send, hist_send, (slab, clus)).wait_send()
    whole_wide(0).wait_send()
    whole_wide(1).wait_send()

    def finish(step, carry):
        whole_two(step).wait_send()

        @pl.when(step < steps - 1)
        def _():
            whole_one(step).wait_send()
            whole_fwd(step, 0).wait_send()
            whole_fwd(step, 1).wait_send()

        return carry

    lax.fori_loop(0, steps, finish, 0)


def local(
    incident, history, near_blocks, near_idx, near_cnt, near_lag, near_frac,
    inverses, rays, shift, far_idx, far_lag, trans,
):
    lags, per, unknowns = history.shape
    steps = incident.shape[0]
    dirs = rays.shape[1]
    slots = near_idx.shape[1]
    far_slots = far_idx.shape[1]
    n_slab = lax.axis_size("slab")
    n_clus = lax.axis_size("clus")
    span = lags + steps
    quarters = dirs // LANES
    slab = lax.axis_index("slab")
    clus = lax.axis_index("clus")
    times = jnp.arange(steps, dtype=jnp.int32)

    past_rays = jnp.einsum("cdu,tcu->tcd", rays, history.astype(jnp.bfloat16), preferred_element_type=jnp.float32)
    past = jnp.sum(past_rays * shift[None], axis=1).reshape(lags, 1, quarters, LANES)
    padded = jnp.pad(history, ((0, 0), (0, 0), (0, 2 * LANES - unknowns)))
    halves = padded.reshape(lags, per, 2, LANES).transpose(0, 2, 1, 3)
    message0 = jnp.concatenate([halves, past], axis=1)

    near_local = near_idx - (slab - 1) * (n_clus * per)
    live = jnp.arange(slots)[None, :] < near_cnt[:, None]
    near_base = (near_local // per) * span + lags - 1 - near_lag
    near_row = (times[:, None] + near_base.reshape(1, -1)).reshape(-1)
    near_sub = (near_local % per).reshape(-1)
    near_now = jnp.where(live, 1.0 - near_frac, 0.0).reshape(-1)
    near_old = jnp.where(live, near_frac, 0.0).reshape(-1)

    def column(table):
        shaped = table.reshape((n_slab, n_clus) + table.shape[1:])
        return lax.dynamic_index_in_dim(shaped, clus, 1, keepdims=False)

    idx, lag, weight = column(far_idx), column(far_lag), column(trans)
    mine = idx // n_clus == slab
    member = idx % n_clus
    old = mine & (lag >= 2)
    base = jnp.where(old, (n_clus + member) * span + lags - lag, n_clus * span)
    far_row = (base.reshape(1, -1) + jnp.where(old.reshape(1, -1), times[:, None], 0)).reshape(-1)
    far_weight = jnp.where(old[..., None], weight.astype(jnp.float32), 0.0).reshape(-1, quarters, LANES)
    newest = mine & (lag == 1)
    onehot = (newest[..., None] & (member[..., None] == jnp.arange(n_clus))).astype(jnp.bfloat16)
    fresh = jnp.einsum("tjm,tjd->mtd", onehot, weight, preferred_element_type=jnp.float32)
    fresh_weight = fresh.reshape(n_clus, n_slab // 2, 2 * quarters, LANES)

    sizes = (steps, lags, n_slab, n_clus, per, slots, unknowns, far_slots)
    smem = pl.BlockSpec(memory_space=pltpu.SMEM)
    vmem = pl.BlockSpec(memory_space=pltpu.VMEM)
    dma = pltpu.SemaphoreType.DMA
    devices = 3 * n_clus
    return pl.pallas_call(
        functools.partial(march, sizes),
        out_shape=jax.ShapeDtypeStruct((steps, per, unknowns), jnp.float32),
        in_specs=[smem] * 5 + [vmem] * 7 + [pl.BlockSpec(memory_space=pl.ANY)],
        out_specs=vmem,
        scratch_shapes=[
            pltpu.VMEM(near_blocks.shape, near_blocks.dtype),
            pltpu.VMEM((devices, span, 3, per, LANES), jnp.float32),
            pltpu.VMEM((steps - 1, devices, 3, per, LANES), jnp.float32),
            pltpu.VMEM((8, LANES), jnp.float32),
            pltpu.VMEM((steps, n_slab, quarters, LANES), jnp.float32),
            pltpu.VMEM((steps, n_slab, quarters, LANES), jnp.float32),
            pltpu.VMEM((n_slab, quarters, LANES), jnp.float32),
            pltpu.VMEM((2, per * slots, LANES), jnp.float32),
            pltpu.VMEM((per, unknowns, LANES), jnp.float32),
            pltpu.VMEM((quarters, LANES), jnp.float32),
            dma(()), dma(()), dma((n_clus,)), dma((2,)), dma((2,)),
            dma((steps - 1,)), dma((steps - 1,)), dma((steps - 1, 2)), dma((steps - 1, 2)),
            dma((steps,)), dma((steps,)),
        ],
        compiler_params=pltpu.CompilerParams(
            collective_id=0, has_side_effects=True, vmem_limit_bytes=48 * 1024 * 1024
        ),
    )(
        near_row, near_sub, near_now, near_old, far_row,
        incident, message0, rays, shift, inverses, far_weight, fresh_weight, near_blocks,
    )


def solution(mesh):
    split = ("slab", "clus")
    in_specs = (
        P(None, split, None),
        P(None, split, None),
        P(split, None, None, None),
        P(split, None),
        P(split),
        P(split, None),
        P(split, None),
        P(split, None, None),
        P(split, None, None),
        P(split, None),
        P(),
        P(),
        P(),
    )
    return jax.shard_map(local, mesh=mesh, in_specs=in_specs, out_specs=P(None, split, None), check_vma=False)
```

time: 1260 us -> 145 us (0.12)
  blocking collectives: 957 us -> 0 us
  Pallas kernels: 0 us -> 133 us
  starting transfers between devices: 81.5 us -> 0 us
  waiting for transfers between devices: 75 us -> 0 us
  local copies, waits for them, and re-layouts: 68.7 us -> 5.49 us
  matrix products: 37.2 us -> 2.74 us
  other arithmetic: 19.7 us -> 3.9 us
  between operations: 14.1 us -> 0.17 us
    all_gather x15 -> x0, blocking collectives: 957 us -> none  [the longest x7 817 us: local(): lax.all_gather(spectrum[None, :], ('slab', 'clus'), axis=0, tiled=True)]
    pallas_call x0 -> x1, Pallas kernels: none -> 133 us  [local(): pl.pallas_call(functools.partial(march, sizes), out_shape=jax.ShapeDtypeS...]
    ppermute x16 -> x0, starting transfers between devices: 81.5 us -> none  [the longest x8 64.9 us: extended(): lax.ppermute(lax.slice_in_dim(block, block.shape[dim] - width, None, axis...]
    all_gather x1 -> x0, waiting for transfers between devices: 64.4 us -> none  [local(): lax.all_gather(own_hist[:, None, :], ('slab', 'clus'), axis=1, tiled=True)]
    gather x40 -> x0, local copies, waits for them, and re-layouts: 44.4 us -> none  [the longest x16 17.1 us: local(): first_lag = near_time[lag_slot, near_local]]
    dot_general x31 -> x1, matrix products: 35.6 us -> 1.37 us  [local(): jnp.einsum('tjm,tjd->mtd', onehot, weight, preferred_element_type=jnp.flo...]
  transfers between devices with their start and end apart: 17 -> 0, of which waited for: 3 -> 0; matrix products, arithmetic and copies ran while one was open for 3% -> 0% of each run, Pallas kernels for 0% -> 0%
where the time goes in v1:
time: 145 us
  Pallas kernels  133 us (92%)
  local copies, waits for them, and re-layouts  5.49 us (4%)
  other arithmetic  3.9 us (3%)
  matrix products  2.74 us (2%)
    pallas_call x1, Pallas kernels, local(): pl.pallas_call(functools.partial(march, sizes), out_shape=jax.ShapeDtypeS...  133 us

profile of v1, /device:TPU:1, one launch (start us, length us, event | category | flops | bytes accessed | tf_op | source)
XLA Modules:
  0.0 144.9 jit_solution(4296187696494709701)
XLA Ops:
  0.0 0.7 add_select_fusion.2
  0.7 0.1 reshape.198.near_sub
  0.8 0.1 add.99
  0.9 0.1 add.102.near_row
  1.0 0.8 fusion.15
  1.7 0.1 reshape.200.near_old
  1.8 0.1 reshape.199.near_now
  1.9 0.9 convert_element_type.13
  2.8 1.4 fusion
  4.2 0.8 reshape.201
  4.9 0.3 fusion.23
  5.2 0.2 copy.30
  5.4 0.1 squeeze.13
  5.5 0.1 copy.35
  5.6 0.8 reshape.202
  6.4 0.3 compare_reduce_fusion
  6.7 0.1 copy.34
  6.8 0.2 copy.31
  7.0 0.1 squeeze.14
  7.1 0.9 pad_bitcast_fusion
  8.0 0.0 copy-start.3
  8.0 1.0 bitcast_convert_fusion
  9.0 0.1 reshape.207
  9.1 0.2 broadcast_select_fusion.far_weight
  9.3 1.4 convolution_bitcast_fusion
  10.7 0.0 copy-start
  10.7 0.0 copy-start.1
  10.7 0.0 copy-start.2
  10.7 0.3 copy.36
  11.1 0.0 copy-done.3
  11.1 0.5 copy.37.rays
  11.6 0.1 copy-done
  11.7 0.0 copy-done.1
  11.7 0.0 copy-done.2
  11.7 132.6 %shard_map.127 = f32[8,4,200]{2,1,0:T(4,128)S(1)} custom-call(s32[384]{0:T(512)S(1)} %add.102.near_row, s32[48]{0:T(128)S(1)} %reshape.198.near_sub, f32[48]{0:T(128)S(1)} %reshape.199.near_now, f32[48]{0:T(128)S(1)} %reshape.200.near_old, s32[1024]{0:T(1024)S(1)} %add_bitcast_fusion.far_row, f32[8,4,200]{2,1,0:T(4,128)S(1)} %copy-done.1, ...), custom_call_target="tpu_custom_call" | custom-call | tf_op jit(solution)/shard_map/pallas_call | solution.py:314
  144.3 0.6 copy.42
  (8 shorter events, 0.1 us)
Async XLA Ops:
  8.0 3.1 %copy-start.3 = (bf16[4,512,200]{1,2,0:T(8,128)(2,1)S(1)}, bf16[4,512,200]{1,2,0:T(8,128)(2,1)}, u32[]{:S(2)}) copy-start(bf16[4,512,200]{1,2,0:T(8,128)(2,1)} %param.21) | copy-start | bytes 2457604
  10.7 1.0 copy-start
  10.7 1.0 copy-start.1
  10.7 1.0 copy-start.2

commit v2 on v1

v2 whole, which is shorter than its diff:
```python
import functools

import jax
import jax.numpy as jnp
from jax import lax
from jax.experimental import pallas as pl
from jax.experimental.pallas import tpu as pltpu
from jax.sharding import PartitionSpec as P

MESH = pl.DeviceIdType.MESH
LANES = 128
CHUNK = 32
SIDE = 4
FAR_FIRST = (
    (2, 2), (2, 1), (2, 3), (1, 2), (3, 2), (2, 0), (0, 2), (1, 1),
    (1, 3), (3, 1), (3, 3), (1, 0), (3, 0), (0, 1), (0, 3),
)
NT = (((1,), (1,)), ((), ()))
NN = (((1,), (0,)), ((), ()))


def dot(left, right, dims):
    return lax.dot_general(left, right, dims, preferred_element_type=jnp.float32)


def remote(src, dst, send, recv, device):
    return pltpu.make_async_remote_copy(
        src_ref=src, dst_ref=dst, send_sem=send, recv_sem=recv,
        device_id=device, device_id_type=MESH,
    )


def march(
    sizes,
    near_idx, near_cnt, near_lag, near_frac, far_code,
    incident, history, rays, shift, inverses, far_weight, fresh_weight, near_hbm,
    out,
    near, line, past, land, part_out, part_in, early, blend, partial, incoming,
    near_sem, ray_send, ray_recv, ray_far_recv, cur_send, cur_recv, cur_far_recv, wide_send, wide_recv,
    one_send, one_recv, fwd_send, fwd_recv, two_send, two_recv,
):
    steps, lags, n_slab, side, per, slots, unknowns, far_slots = sizes
    n_clus = side * side
    middle = lags // 2
    slab = lax.axis_index("slab")
    clus = lax.axis_index("clus")
    row, col = clus // side, lax.rem(clus, side)
    after = lax.rem(slab + 1, n_slab)
    before = lax.rem(slab + n_slab - 1, n_slab)
    tail = unknowns - LANES
    quarters = shift.shape[1] // LANES
    home = n_clus + clus
    early_half, late_half = pl.ds(0, middle), pl.ds(middle, lags - middle)

    barrier = pltpu.get_barrier_semaphore()

    def greet_plane(k, carry):
        pl.semaphore_signal(barrier, inc=1, device_id=(slab, lax.rem(clus + k, n_clus)), device_id_type=MESH)
        return carry

    def greet_column(k, carry):
        pl.semaphore_signal(barrier, inc=1, device_id=(lax.rem(slab + k, n_slab), clus), device_id_type=MESH)
        return carry

    lax.fori_loop(1, n_clus, greet_plane, 0)
    lax.fori_loop(1, n_slab, greet_column, 0)
    fetch = pltpu.make_async_copy(near_hbm, near, near_sem)
    fetch.start()

    line[1, row, col, pl.ds(0, lags), 0] = history[:, :, :LANES]
    line[1, row, col, pl.ds(0, lags), 1] = jnp.concatenate(
        [history[:, :, LANES:], jnp.zeros((lags, per, LANES - tail), jnp.float32)], axis=2)
    spectra = jnp.zeros((lags, quarters * LANES), jnp.float32)
    for c in range(per):
        spectra += dot(history[:, c, :].astype(jnp.bfloat16), rays[c], NT) * shift[c:c + 1, :]
    for q in range(quarters):
        past[row, col, pl.ds(0, lags), q, :] = spectra[:, q * LANES:(q + 1) * LANES]
    pl.semaphore_wait(barrier, n_clus + n_slab - 2)

    def along_x(k):
        return (slab, row * side + lax.rem(col + k, side))

    def along_y(k):
        return (slab, lax.rem(row + k, side) * side + col)

    own_ray = [past.at[row, col, early_half], past.at[row, col, late_half]]
    own_cur = [line.at[1, row, col, early_half], line.at[1, row, col, late_half]]
    row_ray = [past.at[row, :, early_half], past.at[:, col, late_half]]

    def cur_strip(which, place):
        return line.at[1, place, :, early_half] if which == 0 else line.at[1, :, place, late_half]

    toward = [along_x, along_y]
    place = [row, col]
    for own, send, recv in ((own_ray, ray_send, ray_recv), (own_cur, cur_send, cur_recv)):
        for which in range(2):
            for k in (2, 1, 3):
                remote(own[which], own[which], send.at[0, which], recv.at[which], toward[which](k)).start()

    three_ray = [past.at[0, pl.ds(0, side - 1), early_half], past.at[0, pl.ds(0, side - 1), late_half]]
    three_cur = [line.at[1, 0, pl.ds(0, side - 1), early_half], line.at[1, 0, pl.ds(0, side - 1), late_half]]
    strips_ray = [past.at[pl.ds(0, side - 1), :, early_half], past.at[pl.ds(0, side - 1), :, late_half]]
    strips_cur = [line.at[1, pl.ds(0, side - 1), :, early_half], line.at[1, pl.ds(0, side - 1), :, late_half]]

    def waiter(piece, send, recv):
        return remote(piece, piece, send, recv, (slab, clus))

    for which in range(2):
        waiter(three_ray[which], ray_send.at[0, which], ray_recv.at[which]).wait_recv()
        for k in (2, 1, 3):
            remote(row_ray[which], row_ray[which], ray_send.at[1, which], ray_far_recv.at[which],
                   toward[1 - which](k)).start()

    def wide_start(which, spot):
        piece = cur_strip(which, spot)
        for side_of, device, slot in ((0, before, 2), (1, after, 0)):
            target = line.at[slot, spot, :, early_half] if which == 0 else line.at[slot, :, spot, late_half]
            remote(piece, target, wide_send.at[side_of], wide_recv.at[side_of], (device, clus)).start()

    for which in range(2):
        waiter(three_cur[which], cur_send.at[0, which], cur_recv.at[which]).wait_recv()
        strip = cur_strip(which, place[which])
        for k in (2, 1, 3):
            remote(strip, strip, cur_send.at[1, which], cur_far_recv.at[which, place[which]],
                   toward[1 - which](k)).start()
        wide_start(which, place[which])

    def whole_wide(which):
        piece = line.at[0, :, :, pl.ds(0, lags)]
        return waiter(piece, wide_send.at[which], wide_recv.at[which])

    def far_early(step):
        def one(target, carry):
            total = jnp.zeros((quarters, LANES), jnp.float32)
            for slot in range(far_slots):
                entry = target * far_slots + slot
                code = far_code[entry]
                group, lag = lax.div(code, 32), lax.rem(code, 32)
                member = lax.rem(group, n_clus)
                old = lag >= 2
                time = jnp.where(old, step + lags - lag, 0)
                mine = jnp.where(old & (lax.div(group, n_clus) == slab), 1.0, 0.0)
                total += (far_weight[entry] * mine) * past[lax.div(member, side), lax.rem(member, side), time]
            early[target] = total
            return carry

        lax.fori_loop(0, n_slab, one, 0)

    def far_send(step):
        totals = [
            jnp.concatenate([early[2 * p], early[2 * p + 1]], axis=0) for p in range(n_slab // 2)
        ]
        for member in range(n_clus):
            one = past[member // side, member % side, lags - 1 + step]
            both = jnp.concatenate([one, one], axis=0)
            for p in range(n_slab // 2):
                totals[p] += fresh_weight[member, p] * both
        for p in range(n_slab // 2):
            part_out[step, 2 * p] = totals[p][:quarters]
            part_out[step, 2 * p + 1] = totals[p][quarters:]

        def two_start(k, inner):
            target = lax.rem(slab + k, n_slab)
            remote(part_out.at[step, target], part_in.at[step, slab],
                   two_send.at[step], two_recv.at[step], (target, clus)).start()
            return inner

        lax.fori_loop(1, n_slab, two_start, 0)
        part_in[step, slab] = part_out[step, slab]

    for which in range(2):
        waiter(strips_ray[which], ray_send.at[1, which], ray_far_recv.at[which]).wait_recv()
    far_early(0)
    far_send(0)

    for k in (1, 3, 2):
        for which in range(2):
            spot = lax.rem(place[which] + k, side)
            waiter(cur_strip(which, spot), cur_send.at[1, which], cur_far_recv.at[which, spot]).wait_recv()
            wide_start(which, spot)

    whole_wide(0).wait_recv()
    whole_wide(1).wait_recv()
    fetch.wait()

    row_id = lax.broadcasted_iota(jnp.int32, (per, 1), 0)

    def whole_one(step):
        return waiter(land.at[step, pl.ds(0, n_clus - 1)], one_send.at[step], one_recv.at[step])

    def whole_fwd(step, which):
        return waiter(land.at[step, pl.ds(0, n_clus), pl.ds(0, 2)], fwd_send.at[step, which], fwd_recv.at[step, which])

    def whole_two(step):
        return waiter(part_in.at[step, pl.ds(0, n_slab - 1)], two_send.at[step], two_recv.at[step])

    def body(step, carry):
        @pl.when(step > 0)
        def _():
            last = step - 1
            for which, slot in ((0, 2), (1, 0)):
                whole_fwd(last, which).wait_recv()
                for k in range(n_clus):
                    line[slot, k // side, k % side, lags + last] = land[last, slot * n_clus + k, pl.ds(0, 2)]

        def blend_one(c, inner):
            for j in range(slots):
                entry = c * slots + j
                local_idx = jnp.clip(near_idx[c, j] - (slab - 1) * (n_clus * per), 0, 3 * n_clus * per - 1)
                device, sub = lax.div(local_idx, per), lax.rem(local_idx, per)
                spot = lax.rem(device, n_clus)
                index = (lax.div(device, n_clus), lax.div(spot, side), lax.rem(spot, side))
                time = step + lags - 1 - near_lag[c, j]
                live = j < near_cnt[c]
                now = jnp.where(live, 1.0 - near_frac[c, j], 0.0)
                old = jnp.where(live, near_frac[c, j], 0.0)
                for half in range(2):
                    mixed = (
                        now * line[index + (time + 1, half, pl.ds(sub, 1), slice(None))]
                        + old * line[index + (time, half, pl.ds(sub, 1), slice(None))]
                    )
                    blend[half, pl.ds(entry, 1), :] = mixed.astype(jnp.bfloat16).astype(jnp.float32)
            return inner

        lax.fori_loop(0, per, blend_one, 0)

        def near_one(c, inner):
            for first in range(0, unknowns, CHUNK):
                rows = min(CHUNK, unknowns - first)
                left = jnp.zeros((rows, LANES), jnp.float32)
                right = jnp.zeros((rows, tail), jnp.float32)
                for j in range(slots):
                    entry = c * slots + j
                    left += (near[c, j, pl.ds(first, rows), pl.ds(0, LANES)].astype(jnp.float32)
                             * blend[0, pl.ds(entry, 1), :])
                    right += (near[c, j, pl.ds(first, rows), pl.ds(LANES, tail)].astype(jnp.float32)
                              * blend[1, pl.ds(entry, 1), pl.ds(0, tail)])
                partial[c, pl.ds(first, rows), :] = left + jnp.concatenate(
                    [right, jnp.zeros((rows, LANES - tail), jnp.float32)], axis=1)
            return inner

        lax.fori_loop(0, per, near_one, 0)

        field = jnp.zeros((per, unknowns), jnp.float32)
        for c in range(per):
            pick = jnp.where(row_id == c, 1.0, 0.0) * jnp.ones((per, LANES), jnp.float32)
            pick = pick.astype(jnp.bfloat16)
            value = partial[c]
            high = value.astype(jnp.bfloat16)
            low = (value - high.astype(jnp.float32)).astype(jnp.bfloat16)
            field += dot(pick, high, NT) + dot(pick, low, NT)

        whole_two(step).wait_recv()
        incoming[...] = jnp.sum(part_in[step], axis=0)
        spread = jnp.concatenate(
            [shift[:, q * LANES:(q + 1) * LANES] * incoming[pl.ds(q, 1), :] for q in range(quarters)], axis=1)
        for c in range(per):
            field += dot(jnp.where(row_id == c, spread, 0.0).astype(jnp.bfloat16), rays[c], NN)
        right_side = (incident[step] - field).astype(jnp.bfloat16).astype(jnp.float32)
        current = jnp.zeros((per, unknowns), jnp.float32)
        for c in range(per):
            current += dot(jnp.where(row_id == c, right_side, 0.0).astype(jnp.bfloat16), inverses[c], NT)
        out[step] = current

        @pl.when(step < steps - 1)
        def _():
            rounded = current.astype(jnp.bfloat16).astype(jnp.float32)
            values = jnp.zeros((per, quarters * LANES), jnp.float32)
            for c in range(per):
                values += dot(jnp.where(row_id == c, rounded, 0.0).astype(jnp.bfloat16), rays[c], NT)
            spectrum = jnp.sum(values * shift[...], axis=0, keepdims=True)
            land[step, home, 0] = current[:, :LANES]
            land[step, home, 1] = jnp.concatenate(
                [current[:, LANES:], jnp.zeros((per, LANES - tail), jnp.float32)], axis=1)
            for q in range(quarters):
                land[step, home, 2, pl.ds(q, 1), :] = spectrum[:, q * LANES:(q + 1) * LANES]

            for dy, dx in FAR_FIRST:
                piece = land.at[step, home]
                target = lax.rem(row + dy, side) * side + lax.rem(col + dx, side)
                remote(piece, piece, one_send.at[step], one_recv.at[step], (slab, target)).start()

            far_early(step + 1)
            whole_one(step).wait_recv()
            piece = land.at[step, pl.ds(n_clus, n_clus), pl.ds(0, 2)]
            remote(piece, land.at[step, pl.ds(2 * n_clus, n_clus), pl.ds(0, 2)],
                   fwd_send.at[step, 0], fwd_recv.at[step, 0], (before, clus)).start()
            remote(piece, land.at[step, pl.ds(0, n_clus), pl.ds(0, 2)],
                   fwd_send.at[step, 1], fwd_recv.at[step, 1], (after, clus)).start()
            for k in range(n_clus):
                past[k // side, k % side, lags + step] = land[step, n_clus + k, 2]
            far_send(step + 1)
            for k in range(n_clus):
                line[1, k // side, k % side, lags + step] = land[step, n_clus + k, pl.ds(0, 2)]

        return carry

    lax.fori_loop(0, steps, body, 0)

    for which in range(2):
        waiter(three_ray[which], ray_send.at[0, which], ray_recv.at[which]).wait_send()
        waiter(three_cur[which], cur_send.at[0, which], cur_recv.at[which]).wait_send()
        waiter(strips_ray[which], ray_send.at[1, which], ray_recv.at[which]).wait_send()
        waiter(strips_cur[which], cur_send.at[1, which], cur_recv.at[which]).wait_send()
        whole_wide(which).wait_send()

    def finish(step, carry):
        whole_two(step).wait_send()

        @pl.when(step < steps - 1)
        def _():
            whole_one(step).wait_send()
            whole_fwd(step, 0).wait_send()
            whole_fwd(step, 1).wait_send()

        return carry

    lax.fori_loop(0, steps, finish, 0)


def local(
    incident, history, near_blocks, near_idx, near_cnt, near_lag, near_frac,
    inverses, rays, shift, far_idx, far_lag, trans,
):
    lags, per, unknowns = history.shape
    steps = incident.shape[0]
    slots = near_idx.shape[1]
    far_slots = far_idx.shape[1]
    n_slab = lax.axis_size("slab")
    n_clus = lax.axis_size("clus")
    side = SIDE
    span = lags + steps
    quarters = rays.shape[1] // LANES
    slab = lax.axis_index("slab")
    clus = lax.axis_index("clus")

    def column(table):
        shaped = table.reshape((n_slab, n_clus) + table.shape[1:])
        return lax.dynamic_index_in_dim(shaped, clus, 1, keepdims=False)

    code = column(far_idx * 32 + far_lag)
    idx, lag, weight = code // 32, code % 32, column(trans)
    far_weight = weight.astype(jnp.float32).reshape(-1, quarters, LANES)
    newest = (idx // n_clus == slab) & (lag == 1)
    onehot = (newest[..., None] & (idx[..., None] % n_clus == jnp.arange(n_clus))).astype(jnp.bfloat16)
    fresh = jnp.einsum("tjm,tjd->mtd", onehot, weight, preferred_element_type=jnp.float32)
    fresh_weight = fresh.reshape(n_clus, n_slab // 2, 2 * quarters, LANES)

    sizes = (steps, lags, n_slab, side, per, slots, unknowns, far_slots)
    smem = pl.BlockSpec(memory_space=pltpu.SMEM)
    vmem = pl.BlockSpec(memory_space=pltpu.VMEM)
    dma = pltpu.SemaphoreType.DMA
    return pl.pallas_call(
        functools.partial(march, sizes),
        out_shape=jax.ShapeDtypeStruct((steps, per, unknowns), jnp.float32),
        in_specs=[smem] * 5 + [vmem] * 7 + [pl.BlockSpec(memory_space=pl.ANY)],
        out_specs=vmem,
        scratch_shapes=[
            pltpu.VMEM(near_blocks.shape, near_blocks.dtype),
            pltpu.VMEM((3, side, side, span, 2, per, LANES), jnp.float32),
            pltpu.VMEM((side, side, span, quarters, LANES), jnp.float32),
            pltpu.VMEM((steps - 1, 3 * n_clus, 3, per, LANES), jnp.float32),
            pltpu.VMEM((steps, n_slab, quarters, LANES), jnp.float32),
            pltpu.VMEM((steps, n_slab, quarters, LANES), jnp.float32),
            pltpu.VMEM((n_slab, quarters, LANES), jnp.float32),
            pltpu.VMEM((2, per * slots, LANES), jnp.float32),
            pltpu.VMEM((per, unknowns, LANES), jnp.float32),
            pltpu.VMEM((quarters, LANES), jnp.float32),
            dma(()), dma((2, 2)), dma((2,)), dma((2,)), dma((2, 2)), dma((2,)), dma((2, side)), dma((2,)), dma((2,)),
            dma((steps - 1,)), dma((steps - 1,)), dma((steps - 1, 2)), dma((steps - 1, 2)),
            dma((steps,)), dma((steps,)),
        ],
        compiler_params=pltpu.CompilerParams(
            collective_id=0, has_side_effects=True, vmem_limit_bytes=48 * 1024 * 1024
        ),
    )(
        near_idx, near_cnt, near_lag, near_frac, code.reshape(-1),
        incident, history, rays, shift, inverses, far_weight, fresh_weight, near_blocks,
    )


def solution(mesh):
    split = ("slab", "clus")
    in_specs = (
        P(None, split, None),
        P(None, split, None),
        P(split, None, None, None),
        P(split, None),
        P(split),
        P(split, None),
        P(split, None),
        P(split, None, None),
        P(split, None, None),
        P(split, None),
        P(),
        P(),
        P(),
    )
    return jax.shard_map(local, mesh=mesh, in_specs=in_specs, out_specs=P(None, split, None), check_vma=False)
```

time: 145 us -> 122 us (0.84)
  Pallas kernels: 133 us -> 116 us
  local copies, waits for them, and re-layouts: 5.49 us -> 2.43 us
  other arithmetic: 3.9 us -> 1.76 us
    pallas_call x1, Pallas kernels: 133 us -> 116 us  [local(): pl.pallas_call(functools.partial(march, sizes), out_shape=jax.ShapeDtypeS...]
    select_n x5 -> x1, other arithmetic: 1.7 us -> 0.02 us  [local(): idx[..., None] % n_clus == jnp.arange(n_clus)]
    reshape x2 -> x1, local copies, waits for them, and re-layouts: 1.55 us -> 0.08 us  [column(): shaped = table.reshape((n_slab, n_clus) + table.shape[1:])]
where the time goes in v2:
time: 122 us
  Pallas kernels  116 us (95%)
  local copies, waits for them, and re-layouts  2.43 us (2%)
  other arithmetic  1.76 us (1%)
  matrix products  1.37 us (1%)
    pallas_call x1, Pallas kernels, local(): pl.pallas_call(functools.partial(march, sizes), out_shape=jax.ShapeDtypeS...  116 us

profile of v2, /device:TPU:1, one launch (start us, length us, event | category | flops | bytes accessed | tf_op | source)
XLA Modules:
  0.0 121.7 jit_solution(13804412070515136092)
XLA Ops:
  0.0 0.0 copy-start.8
  0.0 0.8 multiply_add_fusion
  0.8 0.1 reshape.109
  0.9 0.3 fusion.14
  1.2 0.2 copy.26
  1.3 0.1 reshape.110.far_code
  1.5 0.1 copy.28
  1.6 0.1 copy.29
  1.6 0.9 bitcast_convert_fusion
  2.6 0.1 reshape.113.far_weight
  2.7 1.4 %convolution_bitcast_fusion = f32[16,16,512]{2,0,1:T(8,128)S(1)} fusion(bf16[16,16,8,512]{3,2,1,0:T(8,128)(2,1)} %bitcast.18, s32[]{:T(128)S(6)} %select_n.47, s32[16,8]{1,0:T(8,128)S(1)} %copy.29, pred[16,8]{1,0:T(8,128)(4,1)S(1)} %copy.28), kind=kOutput, calls=%fused_computation | convolution fusion | flops 2101248 | bytes 656004 | tf_op jit(solution)/shard_map/tjm,tjd->mtd/dot_general | solution.py:346
  4.1 0.0 copy-start
  4.1 0.0 copy-start.1
  4.1 0.0 copy-start.2
  4.1 0.0 copy-start.3
  4.1 0.0 copy-start.4
  4.1 0.0 copy-start.5
  4.1 0.0 copy-start.6
  4.1 0.0 copy-start.7
  4.2 0.3 copy.30
  4.5 0.0 copy-done.8
  4.5 0.5 copy.31.rays
  5.0 0.0 copy-done
  5.1 0.0 copy-done.1
  5.1 0.0 copy-done.2
  5.1 0.0 copy-done.3
  5.1 0.0 copy-done.4
  5.1 0.0 copy-done.5
  5.1 0.0 copy-done.6
  5.1 0.0 copy-done.7
  5.1 116.0 %shard_map.127 = f32[8,4,200]{2,1,0:T(4,128)S(1)} custom-call(s32[4,12]{1,0:T(4,128)S(1)} %copy-done.4, s32[4]{0:T(128)S(1)} %copy-done.7, s32[4,12]{1,0:T(4,128)S(1)} %copy-done.5, f32[4,12]{1,0:T(4,128)S(1)} %copy-done.6, s32[128]{0:T(128)S(1)} %reshape.110.far_code, f32[8,4,200]{2,1,0:T(4,128)S(1)} %copy-done.2, f32[16,4,200]{2,1,0:T(4,128)S(1)} %copy-done.1, ...), custom_call_target="tpu_custom_call" | custom-call | tf_op jit(solution)/shard_map/pallas_call | solution.py:353
  121.1 0.6 copy.34
  (3 shorter events, 0.1 us)
Async XLA Ops:
  0.0 4.5 %copy-start.8 = (bf16[4,512,200]{1,2,0:T(8,128)(2,1)S(1)}, bf16[4,512,200]{1,2,0:T(8,128)(2,1)}, u32[]{:S(2)}) copy-start(bf16[4,512,200]{1,2,0:T(8,128)(2,1)} %param.21) | copy-start | bytes 2457604
  4.1 1.0 copy-start
  4.1 1.0 copy-start.1
  4.1 1.0 copy-start.2
  4.1 1.0 copy-start.3
  4.1 1.0 copy-start.4
  4.1 1.0 copy-start.5
  4.1 1.0 copy-start.6
  4.1 1.0 copy-start.7

commit v3 on v2

--- a/solution.py
+++ b/solution.py
@@ -32,12 +32,13 @@
 
 def march(
     sizes,
-    near_idx, near_cnt, near_lag, near_frac, far_code,
-    incident, history, rays, shift, inverses, far_weight, fresh_weight, near_hbm,
+    near_idx_hbm, near_cnt_hbm, near_lag_hbm, near_frac_hbm, far_idx_hbm, far_lag_hbm,
+    incident_hbm, history_hbm, shift_hbm, near_hbm, rays_hbm, inverses_hbm, trans_hbm,
     out,
-    near, line, past, land, part_out, part_in, early, blend, partial, incoming,
-    near_sem, ray_send, ray_recv, ray_far_recv, cur_send, cur_recv, cur_far_recv, wide_send, wide_recv,
-    one_send, one_recv, fwd_send, fwd_recv, two_send, two_recv,
+    near_idx, near_cnt, near_lag, near_frac, far_idx, far_lag, incident, history, shift,
+    near, rays, inverses, trans, far_weight, fresh_weight, line, past, land, land_ray, part_out, part_in, early, blend, partial, incoming,
+    small_sem, near_sem, rays_sem, inverses_sem, trans_sem, ray_send, ray_recv, ray_far_recv, cur_send, cur_recv, cur_far_recv, wide_send, wide_recv,
+    one_send, one_recv, spec_send, spec_recv, fwd_send, fwd_recv, two_send, two_recv,
 ):
     steps, lags, n_slab, side, per, slots, unknowns, far_slots = sizes
     n_clus = side * side
@@ -62,17 +63,36 @@
         pl.semaphore_signal(barrier, inc=1, device_id=(lax.rem(slab + k, n_slab), clus), device_id_type=MESH)
         return carry
 
+    small = [
+        pltpu.make_async_copy(source, target, small_sem.at[n])
+        for n, (source, target) in enumerate((
+            (history_hbm, history), (shift_hbm, shift), (far_idx_hbm, far_idx), (far_lag_hbm, far_lag),
+            (near_idx_hbm, near_idx), (near_lag_hbm, near_lag), (near_frac_hbm, near_frac),
+            (near_cnt_hbm, near_cnt), (incident_hbm, incident),
+        ))
+    ]
+    for fetch in small:
+        fetch.start()
+    fetch_rays = pltpu.make_async_copy(rays_hbm, rays, rays_sem)
+    fetch_rays.start()
     lax.fori_loop(1, n_clus, greet_plane, 0)
     lax.fori_loop(1, n_slab, greet_column, 0)
-    fetch = pltpu.make_async_copy(near_hbm, near, near_sem)
-    fetch.start()
-
+    for group in range(n_slab):
+        pltpu.make_async_copy(trans_hbm.at[group * n_clus + clus], trans.at[group], trans_sem).start()
+    fetch_inverses = pltpu.make_async_copy(inverses_hbm, inverses, inverses_sem)
+    fetch_inverses.start()
+    fetch_near = pltpu.make_async_copy(near_hbm, near, near_sem)
+    fetch_near.start()
+
+    small[0].wait()
     line[1, row, col, pl.ds(0, lags), 0] = history[:, :, :LANES]
     line[1, row, col, pl.ds(0, lags), 1] = jnp.concatenate(
         [history[:, :, LANES:], jnp.zeros((lags, per, LANES - tail), jnp.float32)], axis=2)
+    small[1].wait()
+    fetch_rays.wait()
     spectra = jnp.zeros((lags, quarters * LANES), jnp.float32)
     for c in range(per):
-        spectra += dot(history[:, c, :].astype(jnp.bfloat16), rays[c], NT) * shift[c:c + 1, :]
+        spectra += dot(history[:, c, :].astype(jnp.bfloat16), rays[c], NN) * shift[c:c + 1, :]
     for q in range(quarters):
         past[row, col, pl.ds(0, lags), q, :] = spectra[:, q * LANES:(q + 1) * LANES]
     pl.semaphore_wait(barrier, n_clus + n_slab - 2)
@@ -92,10 +112,20 @@
 
     toward = [along_x, along_y]
     place = [row, col]
-    for own, send, recv in ((own_ray, ray_send, ray_recv), (own_cur, cur_send, cur_recv)):
+
+    def wide_start(which, spots):
+        cut = early_half if which == 0 else late_half
+        for side_of, device, slot in ((0, before, 2), (1, after, 0)):
+            remote(line.at[(1,) + spots + (cut,)], line.at[(slot,) + spots + (cut,)],
+                   wide_send.at[side_of], wide_recv.at[side_of], (device, clus)).start()
+
+    for own, send, recv in ((own_cur, cur_send, cur_recv), (own_ray, ray_send, ray_recv)):
         for which in range(2):
             for k in (2, 1, 3):
                 remote(own[which], own[which], send.at[0, which], recv.at[which], toward[which](k)).start()
+        if own is own_cur:
+            wide_start(0, (row, col))
+            wide_start(1, (row, col))
 
     three_ray = [past.at[0, pl.ds(0, side - 1), early_half], past.at[0, pl.ds(0, side - 1), late_half]]
     three_cur = [line.at[1, 0, pl.ds(0, side - 1), early_half], line.at[1, 0, pl.ds(0, side - 1), late_half]]
@@ -104,18 +134,6 @@
 
     def waiter(piece, send, recv):
         return remote(piece, piece, send, recv, (slab, clus))
-
-    for which in range(2):
-        waiter(three_ray[which], ray_send.at[0, which], ray_recv.at[which]).wait_recv()
-        for k in (2, 1, 3):
-            remote(row_ray[which], row_ray[which], ray_send.at[1, which], ray_far_recv.at[which],
-                   toward[1 - which](k)).start()
-
-    def wide_start(which, spot):
-        piece = cur_strip(which, spot)
-        for side_of, device, slot in ((0, before, 2), (1, after, 0)):
-            target = line.at[slot, spot, :, early_half] if which == 0 else line.at[slot, :, spot, late_half]
-            remote(piece, target, wide_send.at[side_of], wide_recv.at[side_of], (device, clus)).start()
 
     for which in range(2):
         waiter(three_cur[which], cur_send.at[0, which], cur_recv.at[which]).wait_recv()
@@ -123,7 +141,40 @@
         for k in (2, 1, 3):
             remote(strip, strip, cur_send.at[1, which], cur_far_recv.at[which, place[which]],
                    toward[1 - which](k)).start()
-        wide_start(which, place[which])
+    for which in range(2):
+        waiter(three_ray[which], ray_send.at[0, which], ray_recv.at[which]).wait_recv()
+        for k in (2, 1, 3):
+            remote(row_ray[which], row_ray[which], ray_send.at[1, which], ray_far_recv.at[which],
+                   toward[1 - which](k)).start()
+    for which in range(2):
+        for k in (1, 3, 2):
+            spots = (row, lax.rem(col + k, side)) if which == 0 else (lax.rem(row + k, side), col)
+            wide_start(which, spots)
+
+    small[2].wait()
+    small[3].wait()
+    pltpu.make_async_copy(trans_hbm.at[pl.ds(0, n_slab)], trans, trans_sem).wait()
+
+    def weigh(target, carry):
+        wide = trans[target].astype(jnp.float32)
+        for q in range(quarters):
+            far_weight[pl.ds(target * far_slots, far_slots), q, :] = wide[:, q * LANES:(q + 1) * LANES]
+        tags, weights = [], []
+        for slot in range(far_slots):
+            entry = target * far_slots + slot
+            group = far_idx[slot, target * n_clus + clus]
+            lag = far_lag[slot, target * n_clus + clus]
+            tag = jnp.where((lag == 1) & (lax.div(group, n_clus) == slab), lax.rem(group, n_clus), -1)
+            tags.append(jnp.full((quarters, LANES), tag, jnp.int32))
+            weights.append(far_weight[entry])
+        for member in range(n_clus):
+            total = jnp.zeros((quarters, LANES), jnp.float32)
+            for slot in range(far_slots):
+                total += jnp.where(tags[slot] == member, weights[slot], 0.0)
+            fresh_weight[member, target] = total
+        return carry
+
+    lax.fori_loop(0, n_slab, weigh, 0)
 
     def whole_wide(which):
         piece = line.at[0, :, :, pl.ds(0, lags)]
@@ -134,8 +185,8 @@
             total = jnp.zeros((quarters, LANES), jnp.float32)
             for slot in range(far_slots):
                 entry = target * far_slots + slot
-                code = far_code[entry]
-                group, lag = lax.div(code, 32), lax.rem(code, 32)
+                group = far_idx[slot, target * n_clus + clus]
+                lag = far_lag[slot, target * n_clus + clus]
                 member = lax.rem(group, n_clus)
                 old = lag >= 2
                 time = jnp.where(old, step + lags - lag, 0)
@@ -154,42 +205,45 @@
             one = past[member // side, member % side, lags - 1 + step]
             both = jnp.concatenate([one, one], axis=0)
             for p in range(n_slab // 2):
-                totals[p] += fresh_weight[member, p] * both
+                totals[p] += jnp.concatenate(
+                    [fresh_weight[member, 2 * p], fresh_weight[member, 2 * p + 1]], axis=0) * both
         for p in range(n_slab // 2):
             part_out[step, 2 * p] = totals[p][:quarters]
             part_out[step, 2 * p + 1] = totals[p][quarters:]
 
-        def two_start(k, inner):
+        for k in sorted(range(1, n_slab), key=lambda k: -min(k, n_slab - k)):
             target = lax.rem(slab + k, n_slab)
             remote(part_out.at[step, target], part_in.at[step, slab],
                    two_send.at[step], two_recv.at[step], (target, clus)).start()
-            return inner
-
-        lax.fori_loop(1, n_slab, two_start, 0)
         part_in[step, slab] = part_out[step, slab]
 
+    for k in (1, 3, 2):
+        for which in range(2):
+            spot = lax.rem(place[which] + k, side)
+            waiter(cur_strip(which, spot), cur_send.at[1, which], cur_far_recv.at[which, spot]).wait_recv()
+            wide_start(which, (spot, slice(None)) if which == 0 else (slice(None), spot))
     for which in range(2):
         waiter(strips_ray[which], ray_send.at[1, which], ray_far_recv.at[which]).wait_recv()
     far_early(0)
     far_send(0)
 
-    for k in (1, 3, 2):
-        for which in range(2):
-            spot = lax.rem(place[which] + k, side)
-            waiter(cur_strip(which, spot), cur_send.at[1, which], cur_far_recv.at[which, spot]).wait_recv()
-            wide_start(which, spot)
-
     whole_wide(0).wait_recv()
     whole_wide(1).wait_recv()
-    fetch.wait()
+    fetch_inverses.wait()
+    for n in range(4, 9):
+        small[n].wait()
+    fetch_near.wait()
 
     row_id = lax.broadcasted_iota(jnp.int32, (per, 1), 0)
 
     def whole_one(step):
         return waiter(land.at[step, pl.ds(0, n_clus - 1)], one_send.at[step], one_recv.at[step])
 
+    def whole_spec(step):
+        return waiter(land_ray.at[step, pl.ds(0, n_clus - 1)], spec_send.at[step], spec_recv.at[step])
+
     def whole_fwd(step, which):
-        return waiter(land.at[step, pl.ds(0, n_clus), pl.ds(0, 2)], fwd_send.at[step, which], fwd_recv.at[step, which])
+        return waiter(land.at[step, pl.ds(0, n_clus)], fwd_send.at[step, which], fwd_recv.at[step, which])
 
     def whole_two(step):
         return waiter(part_in.at[step, pl.ds(0, n_slab - 1)], two_send.at[step], two_recv.at[step])
@@ -201,7 +255,7 @@
             for which, slot in ((0, 2), (1, 0)):
                 whole_fwd(last, which).wait_recv()
                 for k in range(n_clus):
-                    line[slot, k // side, k % side, lags + last] = land[last, slot * n_clus + k, pl.ds(0, 2)]
+                    line[slot, k // side, k % side, lags + last] = land[last, slot * n_clus + k]
 
         def blend_one(c, inner):
             for j in range(slots):
@@ -255,7 +309,7 @@
         spread = jnp.concatenate(
             [shift[:, q * LANES:(q + 1) * LANES] * incoming[pl.ds(q, 1), :] for q in range(quarters)], axis=1)
         for c in range(per):
-            field += dot(jnp.where(row_id == c, spread, 0.0).astype(jnp.bfloat16), rays[c], NN)
+            field += dot(jnp.where(row_id == c, spread, 0.0).astype(jnp.bfloat16), rays[c], NT)
         right_side = (incident[step] - field).astype(jnp.bfloat16).astype(jnp.float32)
         current = jnp.zeros((per, unknowns), jnp.float32)
         for c in range(per):
@@ -264,34 +318,40 @@
 
         @pl.when(step < steps - 1)
         def _():
-            rounded = current.astype(jnp.bfloat16).astype(jnp.float32)
-            values = jnp.zeros((per, quarters * LANES), jnp.float32)
-            for c in range(per):
-                values += dot(jnp.where(row_id == c, rounded, 0.0).astype(jnp.bfloat16), rays[c], NT)
-            spectrum = jnp.sum(values * shift[...], axis=0, keepdims=True)
             land[step, home, 0] = current[:, :LANES]
             land[step, home, 1] = jnp.concatenate(
                 [current[:, LANES:], jnp.zeros((per, LANES - tail), jnp.float32)], axis=1)
-            for q in range(quarters):
-                land[step, home, 2, pl.ds(q, 1), :] = spectrum[:, q * LANES:(q + 1) * LANES]
-
             for dy, dx in FAR_FIRST:
                 piece = land.at[step, home]
                 target = lax.rem(row + dy, side) * side + lax.rem(col + dx, side)
                 remote(piece, piece, one_send.at[step], one_recv.at[step], (slab, target)).start()
 
+            rounded = current.astype(jnp.bfloat16).astype(jnp.float32)
+            values = jnp.zeros((per, quarters * LANES), jnp.float32)
+            for c in range(per):
+                values += dot(jnp.where(row_id == c, rounded, 0.0).astype(jnp.bfloat16), rays[c], NN)
+            spectrum = jnp.sum(values * shift[...], axis=0, keepdims=True)
+            for q in range(quarters):
+                land_ray[step, clus, pl.ds(q, 1), :] = spectrum[:, q * LANES:(q + 1) * LANES]
+
+            for dy, dx in FAR_FIRST:
+                piece = land_ray.at[step, clus]
+                target = lax.rem(row + dy, side) * side + lax.rem(col + dx, side)
+                remote(piece, piece, spec_send.at[step], spec_recv.at[step], (slab, target)).start()
+
             far_early(step + 1)
             whole_one(step).wait_recv()
-            piece = land.at[step, pl.ds(n_clus, n_clus), pl.ds(0, 2)]
-            remote(piece, land.at[step, pl.ds(2 * n_clus, n_clus), pl.ds(0, 2)],
+            piece = land.at[step, pl.ds(n_clus, n_clus)]
+            remote(piece, land.at[step, pl.ds(2 * n_clus, n_clus)],
                    fwd_send.at[step, 0], fwd_recv.at[step, 0], (before, clus)).start()
-            remote(piece, land.at[step, pl.ds(0, n_clus), pl.ds(0, 2)],
+            remote(piece, land.at[step, pl.ds(0, n_clus)],
                    fwd_send.at[step, 1], fwd_recv.at[step, 1], (after, clus)).start()
+            whole_spec(step).wait_recv()
             for k in range(n_clus):
-                past[k // side, k % side, lags + step] = land[step, n_clus + k, 2]
+                past[k // side, k % side, lags + step] = land_ray[step, k]
             far_send(step + 1)
             for k in range(n_clus):
-                line[1, k // side, k % side, lags + step] = land[step, n_clus + k, pl.ds(0, 2)]
+                line[1, k // side, k % side, lags + step] = land[step, n_clus + k]
 
         return carry
 
@@ -310,6 +370,7 @@
         @pl.when(step < steps - 1)
         def _():
             whole_one(step).wait_send()
+            whole_spec(step).wait_send()
             whole_fwd(step, 0).wait_send()
             whole_fwd(step, 1).wait_send()
 
@@ -331,51 +392,50 @@
     side = SIDE
     span = lags + steps
     quarters = rays.shape[1] // LANES
-    slab = lax.axis_index("slab")
-    clus = lax.axis_index("clus")
-
-    def column(table):
-        shaped = table.reshape((n_slab, n_clus) + table.shape[1:])
-        return lax.dynamic_index_in_dim(shaped, clus, 1, keepdims=False)
-
-    code = column(far_idx * 32 + far_lag)
-    idx, lag, weight = code // 32, code % 32, column(trans)
-    far_weight = weight.astype(jnp.float32).reshape(-1, quarters, LANES)
-    newest = (idx // n_clus == slab) & (lag == 1)
-    onehot = (newest[..., None] & (idx[..., None] % n_clus == jnp.arange(n_clus))).astype(jnp.bfloat16)
-    fresh = jnp.einsum("tjm,tjd->mtd", onehot, weight, preferred_element_type=jnp.float32)
-    fresh_weight = fresh.reshape(n_clus, n_slab // 2, 2 * quarters, LANES)
-
     sizes = (steps, lags, n_slab, side, per, slots, unknowns, far_slots)
-    smem = pl.BlockSpec(memory_space=pltpu.SMEM)
     vmem = pl.BlockSpec(memory_space=pltpu.VMEM)
     dma = pltpu.SemaphoreType.DMA
     return pl.pallas_call(
         functools.partial(march, sizes),
         out_shape=jax.ShapeDtypeStruct((steps, per, unknowns), jnp.float32),
-        in_specs=[smem] * 5 + [vmem] * 7 + [pl.BlockSpec(memory_space=pl.ANY)],
+        in_specs=[pl.BlockSpec(memory_space=pltpu.HBM)] * 13,
         out_specs=vmem,
         scratch_shapes=[
+            pltpu.SMEM(near_idx.shape, jnp.int32),
+            pltpu.SMEM(near_cnt.shape, jnp.int32),
+            pltpu.SMEM(near_lag.shape, jnp.int32),
+            pltpu.SMEM(near_frac.shape, jnp.float32),
+            pltpu.SMEM(far_idx.shape[::-1], jnp.int32),
+            pltpu.SMEM(far_lag.shape[::-1], jnp.int32),
+            pltpu.VMEM(incident.shape, jnp.float32),
+            pltpu.VMEM(history.shape, jnp.float32),
+            pltpu.VMEM(shift.shape, jnp.float32),
             pltpu.VMEM(near_blocks.shape, near_blocks.dtype),
+            pltpu.VMEM((rays.shape[0],) + rays.shape[:0:-1], rays.dtype),
+            pltpu.VMEM(inverses.shape, inverses.dtype),
+            pltpu.VMEM((n_slab,) + trans.shape[1:], trans.dtype),
+            pltpu.VMEM((n_slab * far_slots, quarters, LANES), jnp.float32),
+            pltpu.VMEM((n_clus, n_slab, quarters, LANES), jnp.float32),
             pltpu.VMEM((3, side, side, span, 2, per, LANES), jnp.float32),
             pltpu.VMEM((side, side, span, quarters, LANES), jnp.float32),
-            pltpu.VMEM((steps - 1, 3 * n_clus, 3, per, LANES), jnp.float32),
+            pltpu.VMEM((steps - 1, 3 * n_clus, 2, per, LANES), jnp.float32),
+            pltpu.VMEM((steps - 1, n_clus, quarters, LANES), jnp.float32),
             pltpu.VMEM((steps, n_slab, quarters, LANES), jnp.float32),
             pltpu.VMEM((steps, n_slab, quarters, LANES), jnp.float32),
             pltpu.VMEM((n_slab, quarters, LANES), jnp.float32),
             pltpu.VMEM((2, per * slots, LANES), jnp.float32),
             pltpu.VMEM((per, unknowns, LANES), jnp.float32),
             pltpu.VMEM((quarters, LANES), jnp.float32),
-            dma(()), dma((2, 2)), dma((2,)), dma((2,)), dma((2, 2)), dma((2,)), dma((2, side)), dma((2,)), dma((2,)),
-            dma((steps - 1,)), dma((steps - 1,)), dma((steps - 1, 2)), dma((steps - 1, 2)),
+            dma((9,)), dma(()), dma(()), dma(()), dma(()), dma((2, 2)), dma((2,)), dma((2,)), dma((2, 2)), dma((2,)), dma((2, side)), dma((2,)), dma((2,)),
+            dma((steps - 1,)), dma((steps - 1,)), dma((steps - 1,)), dma((steps - 1,)), dma((steps - 1, 2)), dma((steps - 1, 2)),
             dma((steps,)), dma((steps,)),
         ],
         compiler_params=pltpu.CompilerParams(
-            collective_id=0, has_side_effects=True, vmem_limit_bytes=48 * 1024 * 1024
+            collective_id=0, has_side_effects=True, vmem_limit_bytes=63 * 1024 * 1024
         ),
     )(
-        near_idx, near_cnt, near_lag, near_frac, code.reshape(-1),
-        incident, history, rays, shift, inverses, far_weight, fresh_weight, near_blocks,
+        near_idx, near_cnt, near_lag, near_frac, far_idx.T, far_lag.T,
+        incident, history, shift, near_blocks, jnp.swapaxes(rays, 1, 2), inverses, trans,
     )
 
 

time: 122 us -> 116 us (0.951)
  other arithmetic: 1.76 us -> 0 us
  matrix products: 1.37 us -> 0 us
    dot_general x1 -> x0, matrix products: 1.37 us -> none  [local(): jnp.einsum('tjm,tjd->mtd', onehot, weight, preferred_element_type=jnp.flo...]
    pallas_call x1, Pallas kernels: 116 us -> 115 us  [local(): pl.pallas_call(functools.partial(march, sizes), out_shape=jax.ShapeDtypeS...]
where the time goes in v3:
time: 116 us
  Pallas kernels  115 us (99%)
  local copies, waits for them, and re-layouts  1.38 us (1%)
    pallas_call x1, Pallas kernels, local(): pl.pallas_call(functools.partial(march, sizes), out_shape=jax.ShapeDtypeS...  115 us

profile of v3, /device:TPU:1, one launch (start us, length us, event | category | flops | bytes accessed | tf_op | source)
XLA Modules:
  0.0 116.1 jit_solution(11541650351480374945)
XLA Ops:
  0.0 114.7 %shard_map.127 = f32[8,4,200]{2,1,0:T(4,128)} custom-call(s32[4,12]{1,0:T(4,128)} %near_idx_hbm.1, s32[4]{0:T(128)} %near_cnt_hbm.1, s32[4,12]{1,0:T(4,128)} %near_lag_hbm.1, f32[4,12]{1,0:T(4,128)} %near_frac_hbm.1, s32[8,256]{1,0:T(8,128)} %bitcast.4, s32[8,256]{1,0:T(8,128)} %bitcast.5, f32[8,4,200]{2,1,0:T(4,128)} %incident_hbm.1, ...), custom_call_target="tpu_custom_call" | custom-call | tf_op jit(solution)/shard_map/pallas_call | solution.py:398
  114.7 1.4 %copy.15 = f32[8,4,200]{2,1,0:T(4,128)} copy(f32[8,4,200]{2,1,0:T(4,128)} %shard_map.127) | data formatting | bytes 51200

commit v4 on v3

--- a/solution.py
+++ b/solution.py
@@ -35,8 +35,8 @@
     near_idx_hbm, near_cnt_hbm, near_lag_hbm, near_frac_hbm, far_idx_hbm, far_lag_hbm,
     incident_hbm, history_hbm, shift_hbm, near_hbm, rays_hbm, inverses_hbm, trans_hbm,
     out,
-    near_idx, near_cnt, near_lag, near_frac, far_idx, far_lag, incident, history, shift,
-    near, rays, inverses, trans, far_weight, fresh_weight, line, past, land, land_ray, part_out, part_in, early, blend, partial, incoming,
+    near_idx, near_cnt, near_lag, near_frac, near_at, near_mix, far_at, far_mine, far_idx, far_lag, incident, history, shift,
+    near, rays, rays_back, inverses, trans, far_weight, fresh_weight, line, past, land, land_ray, part_out, part_in, early, blend, partial, incoming,
     small_sem, near_sem, rays_sem, inverses_sem, trans_sem, ray_send, ray_recv, ray_far_recv, cur_send, cur_recv, cur_far_recv, wide_send, wide_recv,
     one_send, one_recv, spec_send, spec_recv, fwd_send, fwd_recv, two_send, two_recv,
 ):
@@ -119,7 +119,7 @@
             remote(line.at[(1,) + spots + (cut,)], line.at[(slot,) + spots + (cut,)],
                    wide_send.at[side_of], wide_recv.at[side_of], (device, clus)).start()
 
-    for own, send, recv in ((own_cur, cur_send, cur_recv), (own_ray, ray_send, ray_recv)):
+    for own, send, recv in ((own_ray, ray_send, ray_recv), (own_cur, cur_send, cur_recv)):
         for which in range(2):
             for k in (2, 1, 3):
                 remote(own[which], own[which], send.at[0, which], recv.at[which], toward[which](k)).start()
@@ -136,15 +136,15 @@
         return remote(piece, piece, send, recv, (slab, clus))
 
     for which in range(2):
+        waiter(three_ray[which], ray_send.at[0, which], ray_recv.at[which]).wait_recv()
+        for k in (2, 1, 3):
+            remote(row_ray[which], row_ray[which], ray_send.at[1, which], ray_far_recv.at[which],
+                   toward[1 - which](k)).start()
+    for which in range(2):
         waiter(three_cur[which], cur_send.at[0, which], cur_recv.at[which]).wait_recv()
         strip = cur_strip(which, place[which])
         for k in (2, 1, 3):
             remote(strip, strip, cur_send.at[1, which], cur_far_recv.at[which, place[which]],
-                   toward[1 - which](k)).start()
-    for which in range(2):
-        waiter(three_ray[which], ray_send.at[0, which], ray_recv.at[which]).wait_recv()
-        for k in (2, 1, 3):
-            remote(row_ray[which], row_ray[which], ray_send.at[1, which], ray_far_recv.at[which],
                    toward[1 - which](k)).start()
     for which in range(2):
         for k in (1, 3, 2):
@@ -164,6 +164,12 @@
             entry = target * far_slots + slot
             group = far_idx[slot, target * n_clus + clus]
             lag = far_lag[slot, target * n_clus + clus]
+            old = lag >= 2
+            member = lax.rem(group, n_clus)
+            far_at[0, entry] = lax.div(member, side)
+            far_at[1, entry] = lax.rem(member, side)
+            far_at[2, entry] = jnp.where(old, lags - lag, 0)
+            far_mine[entry] = jnp.where(old & (lax.div(group, n_clus) == slab), 1.0, 0.0)
             tag = jnp.where((lag == 1) & (lax.div(group, n_clus) == slab), lax.rem(group, n_clus), -1)
             tags.append(jnp.full((quarters, LANES), tag, jnp.int32))
             weights.append(far_weight[entry])
@@ -176,6 +182,35 @@
 
     lax.fori_loop(0, n_slab, weigh, 0)
 
+    def turn(c, carry):
+        for q in range(quarters):
+            wide = rays[c, :, pl.ds(q * LANES, LANES)].astype(jnp.float32)
+            rays_back[c, pl.ds(q * LANES, LANES), :] = wide.T.astype(jnp.bfloat16)
+        return carry
+
+    lax.fori_loop(0, per, turn, 0)
+
+    for n in range(4, 9):
+        small[n].wait()
+
+    def locate(c, carry):
+        for j in range(slots):
+            entry = c * slots + j
+            local_idx = jnp.clip(near_idx[c, j] - (slab - 1) * (n_clus * per), 0, 3 * n_clus * per - 1)
+            device = lax.div(local_idx, per)
+            spot = lax.rem(device, n_clus)
+            near_at[0, entry] = lax.div(device, n_clus)
+            near_at[1, entry] = lax.div(spot, side)
+            near_at[2, entry] = lax.rem(spot, side)
+            near_at[3, entry] = lax.rem(local_idx, per)
+            near_at[4, entry] = lags - 1 - near_lag[c, j]
+            live = j < near_cnt[c]
+            near_mix[0, entry] = jnp.where(live, 1.0 - near_frac[c, j], 0.0)
+            near_mix[1, entry] = jnp.where(live, near_frac[c, j], 0.0)
+        return carry
+
+    lax.fori_loop(0, per, locate, 0)
+
     def whole_wide(which):
         piece = line.at[0, :, :, pl.ds(0, lags)]
         return waiter(piece, wide_send.at[which], wide_recv.at[which])
@@ -185,13 +220,8 @@
             total = jnp.zeros((quarters, LANES), jnp.float32)
             for slot in range(far_slots):
                 entry = target * far_slots + slot
-                group = far_idx[slot, target * n_clus + clus]
-                lag = far_lag[slot, target * n_clus + clus]
-                member = lax.rem(group, n_clus)
-                old = lag >= 2
-                time = jnp.where(old, step + lags - lag, 0)
-                mine = jnp.where(old & (lax.div(group, n_clus) == slab), 1.0, 0.0)
-                total += (far_weight[entry] * mine) * past[lax.div(member, side), lax.rem(member, side), time]
+                time = step + far_at[2, entry]
+                total += (far_weight[entry] * far_mine[entry]) * past[far_at[0, entry], far_at[1, entry], time]
             early[target] = total
             return carry
 
@@ -217,21 +247,19 @@
                    two_send.at[step], two_recv.at[step], (target, clus)).start()
         part_in[step, slab] = part_out[step, slab]
 
+    for which in range(2):
+        waiter(strips_ray[which], ray_send.at[1, which], ray_far_recv.at[which]).wait_recv()
+    far_early(0)
+    far_send(0)
     for k in (1, 3, 2):
         for which in range(2):
             spot = lax.rem(place[which] + k, side)
             waiter(cur_strip(which, spot), cur_send.at[1, which], cur_far_recv.at[which, spot]).wait_recv()
             wide_start(which, (spot, slice(None)) if which == 0 else (slice(None), spot))
-    for which in range(2):
-        waiter(strips_ray[which], ray_send.at[1, which], ray_far_recv.at[which]).wait_recv()
-    far_early(0)
-    far_send(0)
 
     whole_wide(0).wait_recv()
     whole_wide(1).wait_recv()
     fetch_inverses.wait()
-    for n in range(4, 9):
-        small[n].wait()
     fetch_near.wait()
 
     row_id = lax.broadcasted_iota(jnp.int32, (per, 1), 0)
@@ -260,14 +288,10 @@
         def blend_one(c, inner):
             for j in range(slots):
                 entry = c * slots + j
-                local_idx = jnp.clip(near_idx[c, j] - (slab - 1) * (n_clus * per), 0, 3 * n_clus * per - 1)
-                device, sub = lax.div(local_idx, per), lax.rem(local_idx, per)
-                spot = lax.rem(device, n_clus)
-                index = (lax.div(device, n_clus), lax.div(spot, side), lax.rem(spot, side))
-                time = step + lags - 1 - near_lag[c, j]
-                live = j < near_cnt[c]
-                now = jnp.where(live, 1.0 - near_frac[c, j], 0.0)
-                old = jnp.where(live, near_frac[c, j], 0.0)
+                index = (near_at[0, entry], near_at[1, entry], near_at[2, entry])
+                sub = near_at[3, entry]
+                time = step + near_at[4, entry]
+                now, old = near_mix[0, entry], near_mix[1, entry]
                 for half in range(2):
                     mixed = (
                         now * line[index + (time + 1, half, pl.ds(sub, 1), slice(None))]
@@ -297,19 +321,19 @@
 
         field = jnp.zeros((per, unknowns), jnp.float32)
         for c in range(per):
-            pick = jnp.where(row_id == c, 1.0, 0.0) * jnp.ones((per, LANES), jnp.float32)
+            pick = jnp.where(row_id == c, 1.0, 0.0) * jnp.ones((per, 2 * LANES), jnp.float32)
             pick = pick.astype(jnp.bfloat16)
             value = partial[c]
             high = value.astype(jnp.bfloat16)
             low = (value - high.astype(jnp.float32)).astype(jnp.bfloat16)
-            field += dot(pick, high, NT) + dot(pick, low, NT)
+            field += dot(pick, jnp.concatenate([high, low], axis=1), NT)
 
         whole_two(step).wait_recv()
         incoming[...] = jnp.sum(part_in[step], axis=0)
         spread = jnp.concatenate(
             [shift[:, q * LANES:(q + 1) * LANES] * incoming[pl.ds(q, 1), :] for q in range(quarters)], axis=1)
         for c in range(per):
-            field += dot(jnp.where(row_id == c, spread, 0.0).astype(jnp.bfloat16), rays[c], NT)
+            field += dot(jnp.where(row_id == c, spread, 0.0).astype(jnp.bfloat16), rays_back[c], NN)
         right_side = (incident[step] - field).astype(jnp.bfloat16).astype(jnp.float32)
         current = jnp.zeros((per, unknowns), jnp.float32)
         for c in range(per):
@@ -405,6 +429,10 @@
             pltpu.SMEM(near_cnt.shape, jnp.int32),
             pltpu.SMEM(near_lag.shape, jnp.int32),
             pltpu.SMEM(near_frac.shape, jnp.float32),
+            pltpu.SMEM((5, per * slots), jnp.int32),
+            pltpu.SMEM((2, per * slots), jnp.float32),
+            pltpu.SMEM((3, n_slab * far_slots), jnp.int32),
+            pltpu.SMEM((n_slab * far_slots,), jnp.float32),
             pltpu.SMEM(far_idx.shape[::-1], jnp.int32),
             pltpu.SMEM(far_lag.shape[::-1], jnp.int32),
             pltpu.VMEM(incident.shape, jnp.float32),
@@ -412,6 +440,7 @@
             pltpu.VMEM(shift.shape, jnp.float32),
             pltpu.VMEM(near_blocks.shape, near_blocks.dtype),
             pltpu.VMEM((rays.shape[0],) + rays.shape[:0:-1], rays.dtype),
+            pltpu.VMEM(rays.shape, rays.dtype),
             pltpu.VMEM(inverses.shape, inverses.dtype),
             pltpu.VMEM((n_slab,) + trans.shape[1:], trans.dtype),
             pltpu.VMEM((n_slab * far_slots, quarters, LANES), jnp.float32),

time: 116 us -> 113 us (0.974)
  Pallas kernels: 115 us -> 112 us
    pallas_call x1, Pallas kernels: 115 us -> 112 us  [local(): pl.pallas_call(functools.partial(march, sizes), out_shape=jax.ShapeDtypeS...]
where the time goes in v4:
time: 113 us
  Pallas kernels  112 us (99%)
  local copies, waits for them, and re-layouts  1.38 us (1%)
    pallas_call x1, Pallas kernels, local(): pl.pallas_call(functools.partial(march, sizes), out_shape=jax.ShapeDtypeS...  112 us

profile of v4, /device:TPU:1, one launch (start us, length us, event | category | flops | bytes accessed | tf_op | source)
XLA Modules:
  0.0 113.1 jit_solution(1431522725833813774)
XLA Ops:
  0.0 111.7 %shard_map.127 = f32[8,4,200]{2,1,0:T(4,128)} custom-call(s32[4,12]{1,0:T(4,128)} %near_idx_hbm.1, s32[4]{0:T(128)} %near_cnt_hbm.1, s32[4,12]{1,0:T(4,128)} %near_lag_hbm.1, f32[4,12]{1,0:T(4,128)} %near_frac_hbm.1, s32[8,256]{1,0:T(8,128)} %bitcast.4, s32[8,256]{1,0:T(8,128)} %bitcast.5, f32[8,4,200]{2,1,0:T(4,128)} %incident_hbm.1, ...), custom_call_target="tpu_custom_call" | custom-call | tf_op jit(solution)/shard_map/pallas_call | solution.py:422
  111.7 1.4 %copy.15 = f32[8,4,200]{2,1,0:T(4,128)} copy(f32[8,4,200]{2,1,0:T(4,128)} %shard_map.127) | data formatting | bytes 51200

commit v5 on v4

--- a/solution.py
+++ b/solution.py
@@ -63,6 +63,8 @@
         pl.semaphore_signal(barrier, inc=1, device_id=(lax.rem(slab + k, n_slab), clus), device_id_type=MESH)
         return carry
 
+    lax.fori_loop(1, n_clus, greet_plane, 0)
+    lax.fori_loop(1, n_slab, greet_column, 0)
     small = [
         pltpu.make_async_copy(source, target, small_sem.at[n])
         for n, (source, target) in enumerate((
@@ -75,8 +77,6 @@
         fetch.start()
     fetch_rays = pltpu.make_async_copy(rays_hbm, rays, rays_sem)
     fetch_rays.start()
-    lax.fori_loop(1, n_clus, greet_plane, 0)
-    lax.fori_loop(1, n_slab, greet_column, 0)
     for group in range(n_slab):
         pltpu.make_async_copy(trans_hbm.at[group * n_clus + clus], trans.at[group], trans_sem).start()
     fetch_inverses = pltpu.make_async_copy(inverses_hbm, inverses, inverses_sem)
@@ -119,7 +119,7 @@
             remote(line.at[(1,) + spots + (cut,)], line.at[(slot,) + spots + (cut,)],
                    wide_send.at[side_of], wide_recv.at[side_of], (device, clus)).start()
 
-    for own, send, recv in ((own_ray, ray_send, ray_recv), (own_cur, cur_send, cur_recv)):
+    for own, send, recv in ((own_cur, cur_send, cur_recv), (own_ray, ray_send, ray_recv)):
         for which in range(2):
             for k in (2, 1, 3):
                 remote(own[which], own[which], send.at[0, which], recv.at[which], toward[which](k)).start()
@@ -136,15 +136,15 @@
         return remote(piece, piece, send, recv, (slab, clus))
 
     for which in range(2):
-        waiter(three_ray[which], ray_send.at[0, which], ray_recv.at[which]).wait_recv()
-        for k in (2, 1, 3):
-            remote(row_ray[which], row_ray[which], ray_send.at[1, which], ray_far_recv.at[which],
-                   toward[1 - which](k)).start()
-    for which in range(2):
         waiter(three_cur[which], cur_send.at[0, which], cur_recv.at[which]).wait_recv()
         strip = cur_strip(which, place[which])
         for k in (2, 1, 3):
             remote(strip, strip, cur_send.at[1, which], cur_far_recv.at[which, place[which]],
+                   toward[1 - which](k)).start()
+    for which in range(2):
+        waiter(three_ray[which], ray_send.at[0, which], ray_recv.at[which]).wait_recv()
+        for k in (2, 1, 3):
+            remote(row_ray[which], row_ray[which], ray_send.at[1, which], ray_far_recv.at[which],
                    toward[1 - which](k)).start()
     for which in range(2):
         for k in (1, 3, 2):
@@ -247,15 +247,15 @@
                    two_send.at[step], two_recv.at[step], (target, clus)).start()
         part_in[step, slab] = part_out[step, slab]
 
-    for which in range(2):
-        waiter(strips_ray[which], ray_send.at[1, which], ray_far_recv.at[which]).wait_recv()
-    far_early(0)
-    far_send(0)
     for k in (1, 3, 2):
         for which in range(2):
             spot = lax.rem(place[which] + k, side)
             waiter(cur_strip(which, spot), cur_send.at[1, which], cur_far_recv.at[which, spot]).wait_recv()
             wide_start(which, (spot, slice(None)) if which == 0 else (slice(None), spot))
+    for which in range(2):
+        waiter(strips_ray[which], ray_send.at[1, which], ray_far_recv.at[which]).wait_recv()
+    far_early(0)
+    far_send(0)
 
     whole_wide(0).wait_recv()
     whole_wide(1).wait_recv()

time: 113 us -> 114 us (level)
  no operation moved by 1% of the time
where the time goes in v5:
time: 114 us
  Pallas kernels  112 us (98%)
  local copies, waits for them, and re-layouts  1.38 us (1%)
    pallas_call x1, Pallas kernels, local(): pl.pallas_call(functools.partial(march, sizes), out_shape=jax.ShapeDtypeS...  112 us

profile of v5, /device:TPU:1, one launch (start us, length us, event | category | flops | bytes accessed | tf_op | source)
XLA Modules:
  0.0 113.7 jit_solution(9768429260637764650)
XLA Ops:
  0.0 112.3 %shard_map.127 = f32[8,4,200]{2,1,0:T(4,128)} custom-call(s32[4,12]{1,0:T(4,128)} %near_idx_hbm.1, s32[4]{0:T(128)} %near_cnt_hbm.1, s32[4,12]{1,0:T(4,128)} %near_lag_hbm.1, f32[4,12]{1,0:T(4,128)} %near_frac_hbm.1, s32[8,256]{1,0:T(8,128)} %bitcast.4, s32[8,256]{1,0:T(8,128)} %bitcast.5, f32[8,4,200]{2,1,0:T(4,128)} %incident_hbm.1, ...), custom_call_target="tpu_custom_call" | custom-call | tf_op jit(solution)/shard_map/pallas_call | solution.py:422
  112.3 1.4 %copy.15 = f32[8,4,200]{2,1,0:T(4,128)} copy(f32[8,4,200]{2,1,0:T(4,128)} %shard_map.127) | data formatting | bytes 51200
